TPU v7x, 32 devices: a whole 2x2x4 slice. The times are simulated.
32 devices in a mesh: seq: 8 (over z, x), tp: 4 (over y, core).
Axes of the slice: x: 2, y: 2, z: 4, core: 2. Of those that a mesh axis runs over, the one named last changes fastest.
Arguments:
- tokens: bfloat16 [16384, 1024], P(('seq', 'tp')), may hold values from -6 to 6
- segment_ids: int32 [32, 512], P('seq'), may hold values from 0 to 7, never falling along the last dimension, each value on 1 to 256 neighbouring positions
- qkv_weight: bfloat16 [3, 1024, 1024], P(None, None, 'tp'), may hold values from -0.1875 to 0.1875
- out_weight: bfloat16 [1024, 1024], P('tp'), may hold values from -1.5 to 1.5
- up_weight: bfloat16 [1024, 4096], P(None, 'tp'), may hold values from -0.1875 to 0.1875
- down_weight: bfloat16 [4096, 1024], P('tp'), may hold values from -0.09375 to 0.09375
- gain_attn: float32 [1024], replicated, may hold values from 0.5 to 1.5
- shift_attn: float32 [1024], replicated, may hold values from -3 to 3
- gain_ffn: float32 [1024], replicated, may hold values from 0.5 to 1.5
- shift_ffn: float32 [1024], replicated, may hold values from -3 to 3
- cotangent: bfloat16 [16384, 1024], P(('seq', 'tp')), may hold values from -6 to 6
Outputs:
- mixed: bfloat16 [16384, 1024], P(('seq', 'tp'))
- token_grad: float32 [16384, 1024], P(('seq', 'tp'))
- qkv_grad: float32 [3, 1024, 1024], P(None, 'seq', 'tp')
- out_grad: float32 [1024, 1024], P('tp', 'seq')
- up_grad: float32 [1024, 4096], P('seq', 'tp')
- down_grad: float32 [4096, 1024], P('tp', 'seq')
- norm_grads: float32 [4, 1024], P(None, ('seq', 'tp'))
Inputs may be any that keep to these rules, and one draw needn't show every extreme that they name: `segment_ids`: in each packed row the ids never fall, each segment has 1 to 256 tokens, and some segment has exactly 256.
All inputs are finite; a program needn't handle non-finite values.
Results may differ from a plain program's by a relative error of at most 0.02.
Values may be sent and summed in bfloat16 or wider, within the bound.
No kernel may reach another device: no remote copies, remote signals or barrier semaphores. Data moves between devices by JAX's collectives and lax.ppermute only.
A program may use at most 256 MiB of HBM per device.

v0:
```python
import jax
import jax.numpy as jnp
from jax import lax
from jax.sharding import PartitionSpec as P

HDIM = 64


def normalize(values, gain, shift):
    center = values - jnp.mean(values, axis=-1, keepdims=True)
    spread = jnp.mean(center * center, axis=-1, keepdims=True)
    return center * lax.rsqrt(spread + 1e-12) * gain + shift


def gelu_exact(values):
    return jax.nn.gelu(values, approximate=False)


def scores_of(queries, keys, segments, scale):
    raw = jnp.einsum("rqhd,rkhd->rhqk", queries, keys, preferred_element_type=jnp.float32) * scale
    same = segments[:, None, :, None] == segments[:, None, None, :]
    return jnp.where(same, raw, -1000000000.0)


def attend(queries, keys, values, segments, scale):
    scores = scores_of(queries, keys, segments, scale)
    peak = jnp.max(scores, axis=-1, keepdims=True)
    weights = jnp.exp(scores - peak)
    summed = jnp.sum(weights, axis=-1, keepdims=True)
    probs = weights / summed
    context = jnp.einsum(
        "rhqk,rkhd->rqhd", probs.astype(jnp.bfloat16), values, preferred_element_type=jnp.float32
    )
    return (context.astype(jnp.bfloat16), peak + jnp.log(summed))


def attend_back(queries, keys, values, segments, scale, logsum, d_context):
    scores = scores_of(queries, keys, segments, scale)
    probs = jnp.exp(scores - logsum)
    d_probs = jnp.einsum("rqhd,rkhd->rhqk", d_context, values, preferred_element_type=jnp.float32)
    inner = jnp.sum(probs * d_probs, axis=-1, keepdims=True)
    d_scores = (probs * (d_probs - inner)).astype(jnp.bfloat16)
    d_query = (
        jnp.einsum("rhqk,rkhd->rqhd", d_scores, keys, preferred_element_type=jnp.float32) * scale
    )
    d_key = (
        jnp.einsum("rhqk,rqhd->rkhd", d_scores, queries, preferred_element_type=jnp.float32) * scale
    )
    d_value = jnp.einsum(
        "rhqk,rqhd->rkhd", probs.astype(jnp.bfloat16), d_context, preferred_element_type=jnp.float32
    )
    return jnp.stack([d_query, d_key, d_value]).astype(jnp.bfloat16)


def contract_rows(left, right):
    return lax.dot_general(
        left, right, (((0,), (0,)), ((), ())), preferred_element_type=jnp.float32
    )


def contract_cols(left, right):
    return lax.dot_general(
        left, right, (((1,), (1,)), ((), ())), preferred_element_type=jnp.float32
    )


def body(
    tokens,
    segment_ids,
    qkv_weight,
    out_weight,
    up_weight,
    down_weight,
    gain_attn,
    shift_attn,
    gain_ffn,
    shift_ffn,
    cotangent,
):
    packed = segment_ids.shape[1]
    scale = HDIM ** (-0.5)
    rows_all = lax.all_gather(tokens, "tp", axis=0, tiled=True)
    row_count = rows_all.shape[0]
    blocks_all = row_count // packed
    projected = jnp.einsum(
        "nd,kdc->knc", rows_all, qkv_weight, preferred_element_type=jnp.float32
    ).astype(jnp.bfloat16)
    width = projected.shape[2]
    head_count = width // HDIM
    shaped = projected.reshape(3, blocks_all, packed, head_count, HDIM)
    context, logsum = attend(shaped[0], shaped[1], shaped[2], segment_ids, scale)
    context = context.reshape(row_count, width)
    attn = lax.psum_scatter(
        jnp.dot(context, out_weight, preferred_element_type=jnp.float32).astype(jnp.bfloat16),
        "tp",
        scatter_dimension=0,
        tiled=True,
    ).astype(jnp.float32)
    pre_one = tokens.astype(jnp.float32) + attn
    normed = normalize(pre_one, gain_attn, shift_attn)
    normed_low = normed.astype(jnp.bfloat16)
    normed_all = lax.all_gather(normed_low, "tp", axis=0, tiled=True)
    up_value = jnp.dot(normed_all, up_weight, preferred_element_type=jnp.float32)
    active = gelu_exact(up_value).astype(jnp.bfloat16)
    ffn = lax.psum_scatter(
        jnp.dot(active, down_weight, preferred_element_type=jnp.float32).astype(jnp.bfloat16),
        "tp",
        scatter_dimension=0,
        tiled=True,
    ).astype(jnp.float32)
    pre_two = normed + ffn
    mixed, second_pull = jax.vjp(normalize, pre_two, gain_ffn, shift_ffn)
    d_pre_two, g_gain_ffn, g_shift_ffn = second_pull(cotangent.astype(jnp.float32))
    d_ffn = d_pre_two.astype(jnp.bfloat16)
    d_ffn_all = lax.all_gather(d_ffn, "tp", axis=0, tiled=True)
    down_grad = contract_rows(active, d_ffn_all)
    d_active = contract_cols(d_ffn_all, down_weight)
    unused, gelu_pull = jax.vjp(gelu_exact, up_value)
    d_up = gelu_pull(d_active)[0].astype(jnp.bfloat16)
    up_grad = contract_rows(normed_all, d_up)
    d_normed = lax.psum_scatter(
        contract_cols(d_up, up_weight).astype(jnp.bfloat16), "tp", scatter_dimension=0, tiled=True
    ).astype(jnp.float32)
    d_normed = d_normed + d_pre_two
    unused, first_pull = jax.vjp(normalize, pre_one, gain_attn, shift_attn)
    d_pre_one, g_gain_attn, g_shift_attn = first_pull(d_normed)
    d_attn = d_pre_one.astype(jnp.bfloat16)
    d_attn_all = lax.all_gather(d_attn, "tp", axis=0, tiled=True)
    out_grad = contract_rows(context, d_attn_all)
    d_context = contract_cols(d_attn_all, out_weight).astype(jnp.bfloat16)
    d_context = d_context.reshape(blocks_all, packed, head_count, HDIM)
    d_qkv = attend_back(shaped[0], shaped[1], shaped[2], segment_ids, scale, logsum, d_context)
    d_qkv = d_qkv.reshape(3, row_count, width)
    qkv_grad = jnp.einsum("nd,knc->kdc", rows_all, d_qkv, preferred_element_type=jnp.float32)
    d_tokens = lax.psum_scatter(
        jnp.einsum("knc,kdc->nd", d_qkv, qkv_weight, preferred_element_type=jnp.float32).astype(
            jnp.bfloat16
        ),
        "tp",
        scatter_dimension=0,
        tiled=True,
    ).astype(jnp.float32)
    weight_terms = (qkv_grad, out_grad, up_grad, down_grad)
    token_grad = d_pre_one + d_tokens
    qkv_grad, out_grad, up_grad, down_grad = (
        lax.psum_scatter(
            weight_terms[0].astype(jnp.bfloat16), "seq", scatter_dimension=1, tiled=True
        ).astype(jnp.float32),
        lax.psum_scatter(
            weight_terms[1].astype(jnp.bfloat16), "seq", scatter_dimension=1, tiled=True
        ).astype(jnp.float32),
        lax.psum_scatter(
            weight_terms[2].astype(jnp.bfloat16), "seq", scatter_dimension=0, tiled=True
        ).astype(jnp.float32),
        lax.psum_scatter(
            weight_terms[3].astype(jnp.bfloat16), "seq", scatter_dimension=1, tiled=True
        ).astype(jnp.float32),
    )
    norm_terms = jnp.stack([g_gain_attn, g_shift_attn, g_gain_ffn, g_shift_ffn])
    norm_grads = lax.psum_scatter(norm_terms, ("seq", "tp"), scatter_dimension=1, tiled=True)
    return (
        mixed.astype(jnp.bfloat16),
        token_grad,
        qkv_grad,
        out_grad,
        up_grad,
        down_grad,
        norm_grads,
    )


def solution(mesh):
    return jax.shard_map(
        body,
        mesh=mesh,
        in_specs=(
            P(("seq", "tp"), None),
            P("seq", None),
            P(None, None, "tp"),
            P("tp", None),
            P(None, "tp"),
            P("tp", None),
            P(),
            P(),
            P(),
            P(),
            P(("seq", "tp"), None),
        ),
        out_specs=(
            P(("seq", "tp"), None),
            P(("seq", "tp"), None),
            P(None, "seq", "tp"),
            P("tp", "seq"),
            P("seq", "tp"),
            P("tp", "seq"),
            P(None, ("seq", "tp")),
        ),
        check_vma=False,
    )
```

profile of v0, /device:TPU:0, one launch (start us, length us, event | category | flops | bytes accessed | tf_op | source)
XLA Modules:
  0.0 866.8 jit_solution(17403057232200861671)
XLA Ops:
  8.0 2.4 broadcast_compare_fusion
  10.3 36.5 %all-gather.5.cloned.1.call-done = bf16[2048,1024]{1,0:T(8,128)(2,1)} async-done(((bf16[512,1024]{1,0:T(8,128)(2,1)}), bf16[2048,1024]{1,0:T(8,128)(2,1)}) %all-gather.5.cloned.1.call-update) | async-done | bytes 4194320 | tf_op jit(solution)/shard_map/all_gather | solution.py:82
  46.8 6.1 fusion.19
  54.5 2.6 squeeze.12
  60.5 9.6 %fusion.60 = (f32[4,4,512]{2,1,0:T(4,128)S(1)}, f32[4,4,512,512]{2,3,1,0:T(8,128)}) fusion(bf16[4,512,4,64]{1,0,3,2:T(4,128)(2,1)} %squeeze.14, bf16[4,512,4,64]{1,0,3,2:T(4,128)(2,1)S(1)} %squeeze.13, pred[4,512,512]{1,2,0:T(8,128)(4,1)} %broadcast_compare_fusion), kind=kOutput, calls=%fused_computation.104 | convolution fusion | flops 549445632 | bytes 19955712 | tf_op jit(solution)/shard_map/rqhd,rkhd->rhqk/dot_general | solution.py:20
  70.1 8.3 fusion
  78.4 7.7 fusion.44
  88.2 3.4 convolution_convert_fusion
  91.7 44.6 %reduce-scatter.18.cloned.1.call-done = bf16[512,1024]{1,0:T(8,128)(2,1)} async-done(((bf16[2048,1024]{1,0:T(8,128)(2,1)}), bf16[512,1024]{1,0:T(8,128)(2,1)}) %reduce-scatter.18.cloned.1.call-update) | async-done | bytes 1048592 | tf_op jit(solution)/shard_map/reduce_scatter | solution.py:93
  141.3 34.6 %all-gather.7.cloned.1.call-done = bf16[2048,1024]{1,0:T(8,128)(2,1)} async-done(((bf16[512,1024]{1,0:T(8,128)(2,1)}), bf16[2048,1024]{1,0:T(8,128)(2,1)}) %all-gather.7.cloned.1.call-update) | async-done | bytes 4194320 | tf_op jit(solution)/shard_map/all_gather | solution.py:102
  175.9 25.1 %multiply_convert_fusion.1 = (bf16[2048,1024]{1,0:T(8,128)(2,1)S(1)}, f32[2048,1024]{1,0:T(8,128)}, f32[2048,1024]{1,0:T(8,128)}) fusion(bf16[2048,1024]{1,0:T(8,128)(2,1)} %all-gather.7.cloned.1.call-done, bf16[1024,1024]{1,0:T(8,128)(2,1)S(1)} %copy-done), kind=kOutput, calls=%fused_computation.14 | convolution fusion | flops 4431282176 | bytes 27262976 | tf_op jit(solution)/shard_map/dot_general | solution.py:103
  203.1 6.0 convolution_convert_fusion.2
  209.7 44.2 %reduce-scatter.20.cloned.1.call-done = bf16[512,1024]{1,0:T(8,128)(2,1)} async-done(((bf16[2048,1024]{1,0:T(8,128)(2,1)}), bf16[512,1024]{1,0:T(8,128)(2,1)}) %reduce-scatter.20.cloned.1.call-update) | async-done | bytes 1048592 | tf_op jit(solution)/shard_map/reduce_scatter | solution.py:105
  253.9 2.5 fusion.57
  262.0 34.6 %all-gather.9.cloned.1.call-done = bf16[2048,1024]{1,0:T(8,128)(2,1)} async-done(((bf16[512,1024]{1,0:T(8,128)(2,1)}), bf16[2048,1024]{1,0:T(8,128)(2,1)}) %all-gather.9.cloned.1.call-update) | async-done | bytes 4194320 | tf_op jit(solution)/shard_map/all_gather | solution.py:115
  296.6 12.7 %add_convert_fusion = bf16[2048,1024]{1,0:T(8,128)(2,1)S(1)} fusion(f32[2048,1024]{1,0:T(8,128)} %get-tuple-element.41, f32[2048,1024]{1,0:T(8,128)} %get-tuple-element.48, bf16[2048,1024]{1,0:T(8,128)(2,1)} %all-gather.9.cloned.1.call-done, bf16[1024,1024]{1,0:T(8,128)(2,1)} %param.16), kind=kOutput, calls=%fused_computation.13 | convolution fusion | flops 4324327424 | bytes 27262976 | tf_op jit(solution)/shard_map/dot_general | solution.py:62
  311.4 6.3 convolution_convert_fusion.1
  317.7 44.6 %reduce-scatter.22.cloned.1.call-done = bf16[512,1024]{1,0:T(8,128)(2,1)} async-done(((bf16[2048,1024]{1,0:T(8,128)(2,1)}), bf16[512,1024]{1,0:T(8,128)(2,1)}) %reduce-scatter.22.cloned.1.call-update) | async-done | bytes 1048592 | tf_op jit(solution)/shard_map/reduce_scatter | solution.py:121
  362.4 3.5 multiply_reduce_fusion.1
  369.7 9.4 %convolution_convert_fusion.4 = bf16[1024,1024]{1,0:T(8,128)(2,1)} fusion(bf16[2048,1024]{1,0:T(8,128)(2,1)} %copy-done.25, bf16[2048,1024]{1,0:T(8,128)(2,1)} %all-gather.9.cloned.1.call-done), kind=kOutput, calls=%fused_computation.65 | convolution fusion | flops 4296015872 | bytes 10485760 | tf_op jit(solution)/shard_map/dot_general | solution.py:56
  379.1 4.0 copy.92
  383.1 9.4 %convolution_convert_fusion.5 = bf16[1024,1024]{1,0:T(8,128)(2,1)} fusion(bf16[2048,1024]{1,0:T(8,128)(2,1)} %all-gather.7.cloned.1.call-done, bf16[2048,1024]{1,0:T(8,128)(2,1)} %copy-done.26), kind=kOutput, calls=%fused_computation.66 | convolution fusion | flops 4296015872 | bytes 10485760 | tf_op jit(solution)/shard_map/dot_general | solution.py:56
  393.8 10.3 %all-gather.11.cloned.1.call-done = bf16[2048,1024]{1,0:T(8,128)(2,1)} async-done(((bf16[512,1024]{1,0:T(8,128)(2,1)}), bf16[2048,1024]{1,0:T(8,128)(2,1)}) %all-gather.11.cloned.1.call-update) | async-done | bytes 4194320 | tf_op jit(solution)/shard_map/all_gather | solution.py:128
  404.1 3.6 convolution_convert_fusion.3
  409.7 2.9 copy.63
  412.7 9.7 %fusion.41 = bf16[4,512,4,64]{1,3,2,0:T(8,128)(2,1)} fusion(bf16[4,512,4,64]{1,3,2,0:T(8,128)(2,1)S(1)} %copy.63, f32[4,4,512,512]{2,3,1,0:T(8,128)} %get-tuple-element.47, f32[4,4,512]{2,1,0:T(4,128)S(1)} %bitcast.91), kind=kOutput, calls=%fused_computation.74 | convolution fusion | flops 545783808 | bytes 18907136 | tf_op jit(solution)/shard_map/rhqk,rqhd->rkhd/dot_general | solution.py:49
  422.4 11.0 %multiply_reduce_fusion = (f32[4,4,512]{2,1,0:T(4,128)S(1)}, f32[4,4,512,512]{2,3,1,0:T(8,128)}) fusion(f32[4,4,512,512]{2,3,1,0:T(8,128)} %get-tuple-element.47, f32[4,4,512]{2,1,0:T(4,128)S(1)} %bitcast.92, bf16[4,512,4,64]{1,3,2,0:T(8,128)(2,1)S(1)} %copy.63, bf16[4,512,4,64]{1,0,3,2:T(4,128)(2,1)S(1)} %copy-done.14), kind=kOutput, calls=%fused_computation.1 | convolution fusion | flops 549445632 | bytes 35717120 | tf_op jit(solution)/shard_map/rqhd,rkhd->rhqk/dot_general | solution.py:40
  433.3 12.4 %multiply_convert_fusion = bf16[4,4,512,512]{2,3,1,0:T(8,128)(2,1)S(1)} fusion(f32[4,4,512,512]{2,3,1,0:T(8,128)} %get-tuple-element.50, f32[4,4,512,512]{2,3,1,0:T(8,128)} %get-tuple-element.47, f32[4,4,512]{2,1,0:T(4,128)S(1)} %get-tuple-element.49, f32[4,4,512]{2,1,0:T(4,128)S(1)} %bitcast.93), kind=kLoop, calls=%fused_computation | loop fusion | flops 16777216 | bytes 42008576 | tf_op jit(solution)/shard_map/convert_element_type | solution.py:42
  445.8 3.7 fusion.40
  449.5 2.5 fusion.39
  451.9 4.1 copy.85
  456.1 4.4 reshape.136
  460.4 4.4 convolution_convert_fusion.6
  468.0 4.0 copy.87
  472.1 4.6 reshape.138
  476.6 2.5 copy.86
  479.1 4.4 reshape.137
  483.6 2.3 constant_dynamic-update-slice_fusion.1
  487.0 7.8 fusion.32
  494.7 4.1 copy.88
  498.9 3.2 copy.102
  502.1 7.8 bitcast_convert_fusion
  511.9 34.4 %reduce-scatter.26.cloned.1.call-done = bf16[128,1024]{1,0:T(8,128)(2,1)} async-done(((bf16[1024,1024]{1,0:T(8,128)(2,1)}), bf16[128,1024]{1,0:T(8,128)(2,1)}) %reduce-scatter.26.cloned.1.call-update) | async-done | bytes 262160 | tf_op jit(solution)/shard_map/reduce_scatter | solution.py:152
  548.2 133.4 %reduce-scatter.34.cloned.1.call-done = f32[32,4]{1,0:T(8,128)} async-done(((f32[1024,4]{1,0:T(8,128)}), f32[32,4]{1,0:T(8,128)}) %reduce-scatter.34.cloned.1.call-update) | async-done | bytes 528
  682.9 59.8 %reduce-scatter.30.cloned.1.call-done = bf16[128,256]{1,0:T(8,128)(2,1)} async-done(((bf16[1024,256]{1,0:T(8,128)(2,1)}), bf16[128,256]{1,0:T(8,128)(2,1)}) %reduce-scatter.30.cloned.1.call-update) | async-done | bytes 65552
  744.3 66.0 %reduce-scatter.28.cloned.1.call-done = bf16[128,768]{1,0:T(8,128)(2,1)} async-done(((bf16[1024,768]{1,0:T(8,128)(2,1)}), bf16[128,768]{1,0:T(8,128)(2,1)}) %reduce-scatter.28.cloned.1.call-update) | async-done | bytes 196624
  812.5 43.8 %reduce-scatter.24.cloned.1.call-done = bf16[512,1024]{1,0:T(8,128)(2,1)} async-done(((bf16[2048,1024]{1,0:T(8,128)(2,1)}), bf16[512,1024]{1,0:T(8,128)(2,1)}) %reduce-scatter.24.cloned.1.call-update) | async-done | bytes 1048592 | tf_op jit(solution)/shard_map/reduce_scatter | solution.py:135
  856.3 3.5 convert_add_fusion
  (119 shorter events, 43.5 us)
Async XLA Ops:
  7.2 168.8 %copy-start = (bf16[1024,1024]{1,0:T(8,128)(2,1)S(1)}, bf16[1024,1024]{1,0:T(8,128)(2,1)}, u32[]{:S(2)}) copy-start(bf16[1024,1024]{1,0:T(8,128)(2,1)} %param.15) | copy-start | bytes 6291460
  7.2 39.6 %all-gather.5.cloned.1.call-start = ((), (), s32[]{:S(2)}) async-start(), calls=%async_computation.9 | async-start | bytes 5242880 | tf_op jit(solution)/shard_map/all_gather | solution.py:82
  7.9 128.4 %reduce-scatter.18.cloned.1.call-start = ((), (), s32[]{:S(2)}) async-start(), calls=%async_computation.10 | async-start | bytes 5242880 | tf_op jit(solution)/shard_map/reduce_scatter | solution.py:93
  60.5 9.6 %copy-start.10 = (bf16[4,512,4,64]{1,0,3,2:T(4,128)(2,1)}, bf16[4,512,4,64]{1,0,3,2:T(4,128)(2,1)S(1)}, u32[]{:S(2)}) copy-start(bf16[4,512,4,64]{1,0,3,2:T(4,128)(2,1)S(1)} %squeeze.13) | copy-start | bytes 3145732
  70.1 8.3 copy-start.13
  86.1 2.1 copy-start.19
  87.2 1.0 copy-start.7
  91.6 44.7 %copy-start.1 = (bf16[512,1024]{1,0:T(8,128)(2,1)S(1)}, bf16[512,1024]{1,0:T(8,128)(2,1)}, u32[]{:S(2)}) copy-start(bf16[512,1024]{1,0:T(8,128)(2,1)} %param.11) | copy-start | bytes 3145732
  91.6 48.1 %copy-start.20 = (f32[1024]{0:T(1024)S(1)}, f32[1024]{0:T(1024)}, u32[]{:S(2)}) copy-start(f32[1024]{0:T(1024)} %param.17) | copy-start | bytes 12292
  91.6 48.1 %copy-start.22 = (f32[1024]{0:T(1024)S(1)}, f32[1024]{0:T(1024)}, u32[]{:S(2)}) copy-start(f32[1024]{0:T(1024)} %param.18) | copy-start | bytes 12292
  91.6 84.3 %all-gather.7.cloned.1.call-start = ((), (), s32[]{:S(2)}) async-start(), calls=%async_computation.11 | async-start | bytes 5242880 | tf_op jit(solution)/shard_map/all_gather | solution.py:102
  136.3 3.4 copy-start.2
  141.3 112.6 %reduce-scatter.20.cloned.1.call-start = ((), (), s32[]{:S(2)}) async-start(), calls=%async_computation.12 | async-start | bytes 5242880 | tf_op jit(solution)/shard_map/reduce_scatter | solution.py:105
  175.9 27.2 %copy-start.24 = (bf16[1024,1024]{1,0:T(8,128)(2,1)S(1)}, bf16[1024,1024]{1,0:T(8,128)(2,1)}, u32[]{:S(2)}) copy-start(bf16[1024,1024]{1,0:T(8,128)(2,1)} %param.16) | copy-start | bytes 6291460
  201.1 2.1 copy-start.25
  209.2 47.5 %copy-start.21 = (f32[1024]{0:T(1024)S(1)}, f32[1024]{0:T(1024)}, u32[]{:S(2)}) copy-start(f32[1024]{0:T(1024)} %param.19) | copy-start | bytes 12292
  209.2 48.4 %copy-start.23 = (f32[1024]{0:T(1024)S(1)}, f32[1024]{0:T(1024)}, u32[]{:S(2)}) copy-start(f32[1024]{0:T(1024)} %param.20) | copy-start | bytes 12292
  209.2 87.4 %all-gather.9.cloned.1.call-start = ((), (), s32[]{:S(2)}) async-start(), calls=%async_computation.13 | async-start | bytes 5242880 | tf_op jit(solution)/shard_map/all_gather | solution.py:115
  253.9 2.9 copy-start.17
  259.5 1.3 copy-start.4
  262.0 100.4 %reduce-scatter.22.cloned.1.call-start = ((), (), s32[]{:S(2)}) async-start(), calls=%async_computation.14 | async-start | bytes 5242880 | tf_op jit(solution)/shard_map/reduce_scatter | solution.py:121
  309.4 2.0 copy-start.26
  317.7 86.4 %all-gather.11.cloned.1.call-start = ((), (), s32[]{:S(2)}) async-start(), calls=%async_computation.15 | async-start | bytes 5242880 | tf_op jit(solution)/shard_map/all_gather | solution.py:128
  362.3 3.5 copy-start.3
  362.3 3.5 copy-start.5
  362.4 3.5 copy-start.18
  367.0 1.3 copy-start.6
  369.5 140.5 %reduce-scatter.32.cloned.1.call-start = ((), (), s32[]{:S(2)}) async-start(), calls=%async_computation.20 | async-start | bytes 2359296
  383.1 163.3 %reduce-scatter.26.cloned.1.call-start = ((), (), s32[]{:S(2)}) async-start(), calls=%async_computation.17 | async-start | bytes 2359296 | tf_op jit(solution)/shard_map/reduce_scatter | solution.py:152
  392.6 289.0 %reduce-scatter.34.cloned.1.call-start = ((), (), s32[]{:S(2)}) async-start(), calls=%async_computation.21 | async-start | bytes 540672
  393.7 349.0 %reduce-scatter.30.cloned.1.call-start = ((), (), s32[]{:S(2)}) async-start(), calls=%async_computation.19 | async-start | bytes 589824
  412.6 9.7 %copy-start.14 = (bf16[4,512,4,64]{1,0,3,2:T(4,128)(2,1)S(1)}, bf16[4,512,4,64]{1,0,3,2:T(4,128)(2,1)}, u32[]{:S(2)}) copy-start(bf16[4,512,4,64]{1,0,3,2:T(4,128)(2,1)} %squeeze.12) | copy-start | bytes 3145732
  433.3 12.4 %copy-start.11 = (bf16[4,512,4,64]{1,0,3,2:T(4,128)(2,1)S(1)}, bf16[4,512,4,64]{1,0,3,2:T(4,128)(2,1)}, u32[]{:S(2)}) copy-start(bf16[4,512,4,64]{1,0,3,2:T(4,128)(2,1)} %copy-done.10) | copy-start | bytes 3145732
  445.8 3.7 copy-start.12
  451.9 8.5 copy-start.8
  460.4 4.4 copy-start.16
  465.9 10.8 %copy-start.9 = (bf16[4,512,4,64]{1,3,2,0:T(8,128)(2,1)S(1)}, bf16[4,512,4,64]{1,3,2,0:T(8,128)(2,1)}, u32[]{:S(2)}) copy-start(bf16[4,512,4,64]{1,3,2,0:T(8,128)(2,1)} %fusion.40) | copy-start | bytes 3145732
  479.1 6.8 copy-start.15
  483.6 326.7 %reduce-scatter.28.cloned.1.call-start = ((), (), s32[]{:S(2)}) async-start(), calls=%async_computation.18 | async-start | bytes 1769472
  502.1 354.2 %reduce-scatter.24.cloned.1.call-start = ((), (), s32[]{:S(2)}) async-start(), calls=%async_computation.16 | async-start | bytes 5242880 | tf_op jit(solution)/shard_map/reduce_scatter | solution.py:135
Sparse Core Ops, SparseCore 0:
  9.6 37.1 all-gather.4
  91.7 44.5 reduce-scatter.17
  141.4 34.4 all-gather.6
  209.3 44.5 reduce-scatter.19
  262.1 34.4 all-gather.8
  317.8 44.4 reduce-scatter.21
  369.6 34.4 all-gather.10
  408.0 67.4 reduce-scatter.31
  479.5 66.8 reduce-scatter.25
  548.5 132.9 reduce-scatter.33
  684.9 57.7 reduce-scatter.29
  746.4 63.9 reduce-scatter.27
  812.9 43.4 reduce-scatter.23
where the time goes:
time: 876 us; the launch traced here: 867 us
  waiting for transfers between devices  588 us (67%)
  matrix products  146 us (17%)
  local copies, waits for them, and re-layouts  69.8 us (8%)
  other arithmetic  47.3 us (5%)
  between operations  14.7 us (2%)
    unnamed x17, waiting for transfers between devices  260 us
    reduce_scatter x1, waiting for transfers between devices, body(): lax.psum_scatter(jnp.dot(context, out_weight, preferred_element_type=jnp....  44.6 us
    reduce_scatter x1, waiting for transfers between devices, body(): lax.psum_scatter(contract_cols(d_up, up_weight).astype(jnp.bfloat16), 'tp...  44.6 us
    reduce_scatter x1, waiting for transfers between devices, body(): lax.psum_scatter(jnp.dot(active, down_weight, preferred_element_type=jnp....  44.2 us
    reduce_scatter x1, waiting for transfers between devices, body(): lax.psum_scatter(jnp.einsum('knc,kdc->nd', d_qkv, qkv_weight, preferred_e...  43.8 us
    all_gather x1, waiting for transfers between devices, body(): rows_all = lax.all_gather(tokens, 'tp', axis=0, tiled=True)  36.5 us
    all_gather x1, waiting for transfers between devices, body(): normed_all = lax.all_gather(normed_low, 'tp', axis=0, tiled=True)  34.6 us
    all_gather x1, waiting for transfers between devices, body(): d_ffn_all = lax.all_gather(d_ffn, 'tp', axis=0, tiled=True)  34.6 us
  transfers between devices with their start and end apart: 13, of which 12 were waited for; matrix products, arithmetic and copies ran while one was open for 16% of the time, Pallas kernels for 0%

commit v1 on v0

v1 whole, which is shorter than its diff:
```python
import functools

import jax
import jax.numpy as jnp
from jax import lax
from jax.experimental import pallas as pl
from jax.experimental.pallas import tpu as pltpu
from jax.sharding import PartitionSpec as P

HDIM = 64
LANE = 128
BF = jnp.bfloat16
F32 = jnp.float32
SCALE = HDIM ** (-0.5)
MASKED = -1000000000.0


def dot(left, right):
    return jnp.dot(left, right, preferred_element_type=F32)


def dot_nt(left, right):
    return lax.dot_general(left, right, (((1,), (1,)), ((), ())), preferred_element_type=F32)


def dot_tn(left, right):
    return lax.dot_general(left, right, (((0,), (0,)), ((), ())), preferred_element_type=F32)


def call(kernel, outs, smem, args, name):
    out_shape = [jax.ShapeDtypeStruct(shape, dtype) for shape, dtype in outs]
    specs = [pl.BlockSpec(memory_space=pltpu.SMEM)] * len(smem)
    specs += [pl.BlockSpec(memory_space=pltpu.VMEM)] * len(args)
    return pl.pallas_call(
        kernel,
        out_shape=out_shape,
        in_specs=specs,
        out_specs=[pl.BlockSpec(memory_space=pltpu.VMEM)] * len(outs),
        compiler_params=pltpu.CompilerParams(vmem_limit_bytes=50 * 1024 * 1024),
        name=name,
    )(*smem, *args)


def store_turned(pos_ref, out_ref, values):
    for block in range(values.shape[1] // LANE):
        start = pl.multiple_of(pos_ref[block] * LANE, LANE)
        out_ref[pl.ds(start, LANE), :] = values[:, block * LANE : (block + 1) * LANE].T


def turn_kernel(pos_ref, x_ref, out_ref):
    store_turned(pos_ref, out_ref, x_ref[...])


def mean_of(values):
    return jnp.mean(values, axis=-1, keepdims=True)


def bias_of(seg_col, seg_row):
    return jnp.where(seg_col == seg_row, 0.0, MASKED)


def attn_fwd_kernel(units, first, last, pos_ref, *refs):
    refs = list(refs)
    tokens_ref, col_ref, row_ref = refs[:3]
    del refs[:3]
    weights = [(refs.pop(0), refs.pop(0)) for _ in range(units)]
    acc_ref = None if first else refs.pop(0)
    if last:
        gain_ref, shift_ref = refs.pop(0), refs.pop(0)
    saved = [(refs.pop(0), refs.pop(0), refs.pop(0)) for _ in range(units)]
    tokens = tokens_ref[...]
    bias = bias_of(col_ref[...], row_ref[...])
    lane = lax.broadcasted_iota(jnp.int32, (1, LANE), 1)
    line = lax.broadcasted_iota(jnp.int32, (LANE, 1), 0)
    contexts = []
    for (wqkv_ref, wo_ref), (qkv_ref, ctx_ref, lse_ref) in zip(weights, saved):
        qkv = dot(tokens, wqkv_ref[...]).astype(BF)
        qkv_ref[...] = qkv
        query, key, value = (qkv[:, i * LANE : (i + 1) * LANE] for i in range(3))
        query = query * jnp.asarray(SCALE, BF)
        value_t = value.T
        parts = []
        for head in range(2):
            mine = lane >= HDIM if head else lane < HDIM
            scores = dot_nt(jnp.where(mine, key, jnp.zeros_like(key)), query) + bias
            peak = jnp.max(scores, axis=0, keepdims=True)
            raw = jnp.exp(scores - peak)
            summed = jnp.sum(raw, axis=0, keepdims=True)
            lse_ref[head : head + 1, :] = peak + jnp.log(summed)
            prob = (raw * (1.0 / summed)).astype(BF)
            parts.append(dot(value_t, prob))
        context = jnp.where(line < HDIM, parts[0], parts[1]).astype(BF).T
        ctx_ref[...] = context
        contexts.append(context)
    both = jnp.concatenate(contexts, axis=1)
    total = dot(both, jnp.concatenate([wo[...] for _, wo in weights], axis=0))
    if not first:
        total = total + acc_ref[...]
    if not last:
        refs[0][...] = total
        return
    hat_ref, inv_ref, low_ref, turned_ref = refs
    pre = tokens.astype(F32) + total
    center = pre - mean_of(pre)
    inv = lax.rsqrt(mean_of(center * center) + 1e-12)
    hat = center * inv
    hat_ref[...] = hat
    inv_ref[...] = jnp.broadcast_to(inv, inv_ref.shape)
    low = (hat * gain_ref[...] + shift_ref[...]).astype(BF)
    low_ref[...] = low
    store_turned(pos_ref, turned_ref, low)


def ffn_fwd_kernel(units, first, last, pos_ref, *refs):
    refs = list(refs)
    low_ref = refs.pop(0)
    weights = [(refs.pop(0), refs.pop(0)) for _ in range(units)]
    acc_ref = None if first else refs.pop(0)
    if last:
        hat_ref, gain1_ref, shift1_ref, gain2_ref, shift2_ref, cot_ref = refs[:6]
        del refs[:6]
    saved = [(refs.pop(0), refs.pop(0)) for _ in range(units)]
    low = low_ref[...]
    total = None
    for (wu_ref, wd_ref), (act_ref, slope_ref) in zip(weights, saved):
        up = dot(low, wu_ref[...])
        phi_big = 0.5 + 0.5 * lax.erf(up * (0.5 ** 0.5))
        phi_small = jnp.exp(up * up * -0.5) * 0.3989422804014327
        slope_ref[...] = phi_big + up * phi_small
        act = (up * phi_big).astype(BF)
        act_ref[...] = act
        part = dot(act, wd_ref[...])
        total = part if total is None else total + part
    if not first:
        total = total + acc_ref[...]
    if not last:
        refs[0][...] = total
        return
    mixed_ref, dpre_ref, dffn_ref, turned_ref, gg_ref, gs_ref = refs
    gain2 = gain2_ref[...]
    pre = hat_ref[...] * gain1_ref[...] + shift1_ref[...] + total
    center = pre - mean_of(pre)
    inv = lax.rsqrt(mean_of(center * center) + 1e-12)
    hat = center * inv
    mixed_ref[...] = (hat * gain2 + shift2_ref[...]).astype(BF)
    cot = cot_ref[...].astype(F32)
    gg_ref[...] = jnp.sum(cot * hat, axis=0, keepdims=True)
    gs_ref[...] = jnp.sum(cot, axis=0, keepdims=True)
    scaled = cot * gain2
    dpre = (scaled - mean_of(scaled) - hat * mean_of(scaled * hat)) * inv
    dpre_ref[...] = dpre
    dffn = dpre.astype(BF)
    dffn_ref[...] = dffn
    store_turned(pos_ref, turned_ref, dffn)


def ffn_bwd_kernel(has_recv, last, pos_ref, *refs):
    refs = list(refs)
    dffn_ref, dffn_t_ref, low_t_ref = refs[:3]
    del refs[:3]
    weights = [[refs.pop(0) for _ in range(4)] for _ in range(2)]
    acc_ref = refs.pop(0)
    recv = [[refs.pop(0) for _ in range(3)] for _ in range(2)] if has_recv else None
    if last:
        hat_ref, inv_ref, gain_ref = refs[:3]
        del refs[:3]
    outs = [[refs.pop(0) for _ in range(3)] for _ in range(2)]
    dffn, dffn_t, low_t = dffn_ref[...], dffn_t_ref[...], low_t_ref[...]
    half = low_t.shape[0] // 2
    total = acc_ref[...]
    for unit in range(2):
        wu_ref, wd_ref, act_ref, slope_ref = weights[unit]
        down_ref, lo_ref, hi_ref = outs[unit]
        d_up = (dot_nt(dffn, wd_ref[...]) * slope_ref[...]).astype(BF)
        total = total + dot_nt(d_up, wu_ref[...])
        down = dot(dffn_t, act_ref[...])
        up_hi = dot(low_t[half:], d_up)
        up_lo = dot(low_t[:half], d_up)
        if has_recv:
            down = down + recv[unit][0][...].astype(F32)
            up_lo = up_lo + recv[unit][1][...].astype(F32)
            up_hi = up_hi + recv[unit][2][...].astype(F32)
        down_ref[...] = down.astype(BF)
        lo_ref[...] = up_lo.astype(BF)
        hi_ref[...] = up_hi.astype(BF)
    if not last:
        refs[0][...] = total
        return
    dpre_ref, datt_ref, turned_ref, gg_ref, gs_ref = refs
    hat = hat_ref[...]
    gg_ref[...] = jnp.sum(total * hat, axis=0, keepdims=True)
    gs_ref[...] = jnp.sum(total, axis=0, keepdims=True)
    scaled = total * gain_ref[...]
    inv = inv_ref[:, :1]
    dpre = (scaled - mean_of(scaled) - hat * mean_of(scaled * hat)) * inv
    dpre_ref[...] = dpre
    datt = dpre.astype(BF)
    datt_ref[...] = datt
    store_turned(pos_ref, turned_ref, datt)


def attn_bwd_kernel(has_recv, *refs):
    refs = list(refs)
    datt_ref, datt_t_ref, tok_t_ref, col_ref, row_ref = refs[:5]
    del refs[:5]
    units = [[refs.pop(0) for _ in range(5)] for _ in range(2)]
    acc_ref = refs.pop(0)
    recv = [[refs.pop(0) for _ in range(3)] for _ in range(2)] if has_recv else None
    outs = [[refs.pop(0) for _ in range(3)] for _ in range(2)]
    out_acc_ref = refs.pop(0)
    datt, datt_t, tok_t = datt_ref[...], datt_t_ref[...], tok_t_ref[...]
    half = tok_t.shape[0] // 2
    bias = bias_of(col_ref[...], row_ref[...])
    lane = lax.broadcasted_iota(jnp.int32, (1, LANE), 1)
    line = lax.broadcasted_iota(jnp.int32, (LANE, 1), 0)
    wo = jnp.concatenate([unit[1][...] for unit in units], axis=0)
    dctx_all = dot_nt(datt, wo).astype(BF)
    grads = []
    for index, (wqkv_ref, wo_ref, qkv_ref, ctx_ref, lse_ref) in enumerate(units):
        dctx = dctx_all[:, index * LANE : (index + 1) * LANE]
        query, key, value = (qkv_ref[:, i * LANE : (i + 1) * LANE] for i in range(3))
        query = query * jnp.asarray(SCALE, BF)
        key_t = key.T
        parts = []
        for head in range(2):
            mine = lane >= HDIM if head else lane < HDIM
            scores = dot_nt(jnp.where(mine, key, jnp.zeros_like(key)), query) + bias
            prob = jnp.exp(scores - lse_ref[head : head + 1, :])
            d_prob = dot_nt(jnp.where(mine, value, jnp.zeros_like(value)), dctx)
            inner = jnp.sum(prob * d_prob, axis=0, keepdims=True)
            d_scores = (prob * (d_prob - inner)).astype(BF)
            parts.append(
                (dot(key_t, d_scores), dot(d_scores, query), dot(prob.astype(BF), dctx))
            )
        d_query = (jnp.where(line < HDIM, parts[0][0], parts[1][0]) * SCALE).astype(BF).T
        d_key = jnp.where(lane < HDIM, parts[0][1], parts[1][1]).astype(BF)
        d_value = jnp.where(lane < HDIM, parts[0][2], parts[1][2]).astype(BF)
        grads.append(jnp.concatenate([d_query, d_key, d_value], axis=1))
    both = jnp.concatenate(grads, axis=1)
    wqkv = jnp.concatenate([unit[0][...] for unit in units], axis=1)
    out_acc_ref[...] = acc_ref[...] + dot_nt(both, wqkv)
    ctx = jnp.concatenate([unit[3][...] for unit in units], axis=1)
    qkv_grad = dot(tok_t, both)
    out_grad = dot(datt_t, ctx)
    for unit in range(2):
        qk_ref, lo_ref, hi_ref = outs[unit]
        qk = qkv_grad[:, unit * 3 * LANE : (unit * 3 + 2) * LANE]
        vo = jnp.concatenate(
            [
                qkv_grad[:, (unit * 3 + 2) * LANE : (unit * 3 + 3) * LANE],
                out_grad[:, unit * LANE : (unit + 1) * LANE],
            ],
            axis=1,
        )
        lo, hi = vo[:half], vo[half:]
        if has_recv:
            qk = qk + recv[unit][0][...].astype(F32)
            lo = lo + recv[unit][1][...].astype(F32)
            hi = hi + recv[unit][2][...].astype(F32)
        qk_ref[...] = qk.astype(BF)
        lo_ref[...] = lo.astype(BF)
        hi_ref[...] = hi.astype(BF)


def swap(value, axis, bit):
    count = lax.axis_size(axis)
    return lax.ppermute(value, axis, [(i, i ^ bit) for i in range(count)])


def add(*values):
    total = values[0].astype(F32)
    for value in values[1:]:
        total = total + value.astype(F32)
    return total.astype(BF)


def body(
    tokens,
    segment_ids,
    qkv_weight,
    out_weight,
    up_weight,
    down_weight,
    gain_attn,
    shift_attn,
    gain_ffn,
    shift_ffn,
    cotangent,
):
    count, width = tokens.shape
    seq, tp = lax.axis_size("seq"), lax.axis_size("tp")
    me_seq, me_tp = lax.axis_index("seq"), lax.axis_index("tp")
    blocks = width // LANE
    fast = seq == blocks and seq == 8 and tp == 4 and qkv_weight.shape[2] == 2 * LANE
    hidden = up_weight.shape[1] * tp // blocks
    seg = lax.dynamic_slice_in_dim(segment_ids, me_tp, 1, axis=0)
    seg_col = seg.reshape(count, 1)
    gains = [g.reshape(1, width) for g in (gain_attn, shift_attn, gain_ffn, shift_ffn)]
    absolute = jnp.arange(blocks, dtype=jnp.int32)
    side = lax.rem(me_seq, 2)
    if fast:
        rel = absolute ^ me_seq
        pos = (rel & 1) * 4 + ((rel >> 1) & 1) * 2 + (rel >> 2)

        def cut(half):
            at = lax.rem(side + half, 2)
            qkv = lax.dynamic_slice_in_dim(qkv_weight, at * LANE, LANE, axis=2)
            return (
                jnp.concatenate([qkv[0], qkv[1], qkv[2]], axis=1),
                lax.dynamic_slice_in_dim(out_weight, at * LANE, LANE, axis=0),
                lax.dynamic_slice_in_dim(up_weight, at * hidden, hidden, axis=1),
                lax.dynamic_slice_in_dim(down_weight, at * hidden, hidden, axis=0),
            )

        units = {(0, 0): cut(0), (0, 1): cut(1)}
        units[2, 0] = tuple(swap(w, "tp", 2) for w in units[0, 0])
        units[1, 0] = tuple(swap(w, "tp", 1) for w in units[0, 0])
        units[1, 1] = tuple(swap(w, "tp", 1) for w in units[0, 1])
        units[2, 1] = tuple(swap(w, "seq", 1) for w in units[2, 0])
        units[3, 0] = tuple(swap(w, "tp", 1) for w in units[2, 0])
        units[3, 1] = tuple(swap(w, "tp", 1) for w in units[2, 1])
    else:
        pos = absolute
        qkv_all = lax.all_gather(qkv_weight, "tp", axis=2, tiled=True)
        out_all = lax.all_gather(out_weight, "tp", axis=0, tiled=True)
        up_all = lax.all_gather(up_weight, "tp", axis=1, tiled=True)
        down_all = lax.all_gather(down_weight, "tp", axis=0, tiled=True)
        units = {}
        for index in range(blocks):
            cols = slice(index * LANE, (index + 1) * LANE)
            hid = slice(index * hidden, (index + 1) * hidden)
            units[index // 2, index % 2] = (
                jnp.concatenate([qkv_all[i][:, cols] for i in range(3)], axis=1),
                out_all[cols],
                up_all[:, hid],
                down_all[hid],
            )
    pairs = blocks // 2
    if fast:
        groups = [[(0, 0), (0, 1)], [(1, 0), (1, 1)], [(2, 0), (3, 0)], [(2, 1), (3, 1)]]
    else:
        groups = [[(j, 0), (j, 1)] for j in range(pairs)]
    wide = (count, width)

    tok_t = call(turn_kernel, [((width, count), BF)], [pos], [tokens], "turn")[0]
    kept = {}
    total = None
    for number, group in enumerate(groups):
        first, last = number == 0, number == len(groups) - 1
        args = [tokens, seg_col, seg]
        for unit in group:
            args += units[unit][:2]
        if not first:
            args.append(total)
        if last:
            args += gains[:2]
        outs = []
        for unit in group:
            outs += [((count, 3 * LANE), BF), ((count, LANE), BF), ((2, count), F32)]
        if last:
            outs += [(wide, F32), ((count, LANE), F32), (wide, BF), ((width, count), BF)]
        else:
            outs.append((wide, F32))
        res = call(
            functools.partial(attn_fwd_kernel, len(group), first, last),
            outs, [pos], args, f"attn_fwd{number}",
        )
        for index, unit in enumerate(group):
            kept[unit] = tuple(res[index * 3 : index * 3 + 3])
        if last:
            hat, inv, low, low_t = res[-4:]
        else:
            total = res[-1]

    acts = {}
    for number, group in enumerate(groups):
        first, last = number == 0, number == len(groups) - 1
        args = [low]
        for unit in group:
            args += units[unit][2:]
        if not first:
            args.append(total)
        if last:
            args += [hat, *gains, cotangent]
        outs = []
        for unit in group:
            outs += [((count, hidden), BF), ((count, hidden), F32)]
        if last:
            outs += [
                (wide, BF), (wide, F32), (wide, BF), ((width, count), BF),
                ((1, width), F32), ((1, width), F32),
            ]
        else:
            outs.append((wide, F32))
        res = call(
            functools.partial(ffn_fwd_kernel, len(group), first, last),
            outs, [pos], args, f"ffn_fwd{number}",
        )
        for index, unit in enumerate(group):
            acts[unit] = tuple(res[index * 2 : index * 2 + 2])
        if last:
            mixed, d_pre, d_ffn, d_ffn_t, g_gain2, g_shift2 = res[-6:]
        else:
            total = res[-1]

    half = width // 2
    order = [3, 2, 1, 0] if fast else list(range(pairs))
    ffn_g, attn_g = {}, {}
    total = d_pre
    for number, j in enumerate(order):
        last = number == len(order) - 1
        args = [d_ffn, d_ffn_t, low_t]
        for h in range(2):
            args += [*units[j, h][2:], *acts[j, h]]
        args.append(total)
        recv = [swap(g, "tp", 1) for g in ffn_g[j + 1]] if fast and j % 2 == 0 else []
        args += recv
        outs = [((width, hidden), BF), ((half, hidden), BF), ((half, hidden), BF)] * 2
        if last:
            args += [hat, inv, gains[0]]
            outs = outs + [
                (wide, F32), (wide, BF), ((width, count), BF), ((1, width), F32), ((1, width), F32),
            ]
        else:
            outs = outs + [(wide, F32)]
        res = call(
            functools.partial(ffn_bwd_kernel, bool(recv), last), outs, [pos], args, f"ffn_bwd{j}"
        )
        ffn_g[j] = res[:6]
        if last:
            d_pre_one, d_att, d_att_t, g_gain1, g_shift1 = res[6:]
        else:
            total = res[6]

    norm_terms = jnp.concatenate([g_gain1, g_shift1, g_gain2, g_shift2], axis=0)
    norm_grads = lax.psum_scatter(norm_terms, ("seq", "tp"), scatter_dimension=1, tiled=True)

    total = d_pre_one
    for j in order:
        args = [d_att, d_att_t, tok_t, seg_col, seg]
        for h in range(2):
            args += [*units[j, h][:2], *kept[j, h]]
        args.append(total)
        recv = [swap(g, "tp", 1) for g in attn_g[j + 1]] if fast and j % 2 == 0 else []
        args += recv
        outs = [((width, 2 * LANE), BF), ((half, 2 * LANE), BF), ((half, 2 * LANE), BF)] * 2
        outs = outs + [(wide, F32)]
        res = call(
            functools.partial(attn_bwd_kernel, bool(recv)), outs, [], args, f"attn_bwd{j}"
        )
        attn_g[j], total = res[:6], res[6]
    token_grad = total

    if fast:
        quarter, eighth = half // 2, half // 4

        def finish(lo):
            lo = [add(g[:quarter], swap(g[quarter:], "seq", 2)) for g in lo]
            return [
                g[:eighth].astype(F32) + swap(g[eighth:], "seq", 4).astype(F32) for g in lo
            ]

        def reduced(far, near):
            first = [swap(far[i], "tp", 2) for i in (0, 3)]
            lo = [add(near[i][:half], r[:half]) for i, r in zip((0, 3), first)]
            hi = [swap(add(near[i][half:], r[half:]), "seq", 1) for i, r in zip((0, 3), first)]
            one = finish([add(lo[0], hi[1]), add(lo[1], hi[0])])
            far_hi = [swap(far[i], "seq", 1) for i in (2, 5)]
            near_hi = [swap(near[i], "seq", 1) for i in (2, 5)]
            far_lo = [add(far[1], far_hi[1]), add(far[4], far_hi[0])]
            far_lo = [swap(g, "tp", 2) for g in far_lo]
            two = finish(
                [add(near[1], near_hi[1], far_lo[0]), add(near[4], near_hi[0], far_lo[1])]
            )
            return one, two

        def ordered(a, b):
            return jnp.where(side == 0, jnp.concatenate([a, b], 1), jnp.concatenate([b, a], 1))

        down, up = reduced(ffn_g[2], ffn_g[0])
        qk, vo = reduced(attn_g[2], attn_g[0])
        down_grad = ordered(*down).T
        up_grad = ordered(*up)
        qkv_grad = jnp.stack(
            [
                ordered(qk[0][:, :LANE], qk[1][:, :LANE]),
                ordered(qk[0][:, LANE:], qk[1][:, LANE:]),
                ordered(vo[0][:, :LANE], vo[1][:, :LANE]),
            ]
        )
        out_grad = ordered(vo[0][:, LANE:], vo[1][:, LANE:]).T
    else:

        def joined(parts):
            return jnp.concatenate(parts, axis=1)

        def scattered(value, tp_dim, seq_dim):
            value = lax.psum_scatter(value, "tp", scatter_dimension=tp_dim, tiled=True)
            value = lax.psum_scatter(value, "seq", scatter_dimension=seq_dim, tiled=True)
            return value.astype(F32)

        both = [(j, h) for j in range(pairs) for h in (0, 3)]

        def whole(g, j, h):
            return jnp.concatenate([g[j][h + 1], g[j][h + 2]], axis=0)

        down_grad = scattered(joined([ffn_g[j][h] for j, h in both]), 1, 0).T
        up_grad = scattered(joined([whole(ffn_g, j, h) for j, h in both]), 1, 0)
        qk = [attn_g[j][h] for j, h in both]
        vo = [whole(attn_g, j, h) for j, h in both]
        qkv_grad = jnp.stack(
            [
                joined([g[:, :LANE] for g in qk]),
                joined([g[:, LANE:] for g in qk]),
                joined([g[:, :LANE] for g in vo]),
            ]
        )
        qkv_grad = scattered(qkv_grad, 2, 1)
        out_grad = scattered(joined([g[:, LANE:] for g in vo]), 1, 0).T
    return (mixed, token_grad, qkv_grad, out_grad, up_grad, down_grad, norm_grads)


def solution(mesh):
    return jax.shard_map(
        body,
        mesh=mesh,
        in_specs=(
            P(("seq", "tp"), None),
            P("seq", None),
            P(None, None, "tp"),
            P("tp", None),
            P(None, "tp"),
            P("tp", None),
            P(),
            P(),
            P(),
            P(),
            P(("seq", "tp"), None),
        ),
        out_specs=(
            P(("seq", "tp"), None),
            P(("seq", "tp"), None),
            P(None, "seq", "tp"),
            P("tp", "seq"),
            P("seq", "tp"),
            P("tp", "seq"),
            P(None, ("seq", "tp")),
        ),
        check_vma=False,
    )
```

time: 876 us -> 604 us (0.69)
  waiting for transfers between devices: 588 us -> 312 us
  Pallas kernels: 0 us -> 150 us
  matrix products: 146 us -> 0 us
  starting transfers between devices: 1.11 us -> 51.9 us
  other arithmetic: 47.3 us -> 16.1 us
  local copies, waits for them, and re-layouts: 69.8 us -> 48.9 us
    reduce_scatter x5 -> x0, waiting for transfers between devices: 212 us -> none  [the longest x1 44.6 us: body(): lax.psum_scatter(jnp.dot(context, out_weight, preferred_element_type=jnp....]
    ppermute x0 -> x84, waiting for transfers between devices: none -> 181 us  [swap(): return lax.ppermute(value, axis, [(i, i ^ bit) for i in range(count)])]
    pallas_call x0 -> x17, Pallas kernels: none -> 150 us  [call(): pl.pallas_call(kernel, out_shape=out_shape, in_specs=specs, out_specs=[pl...]
    dot_general x18 -> x0, matrix products: 146 us -> none  [the longest x1 25.1 us: body(): jnp.dot(normed_all, up_weight, preferred_element_type=jnp.float32)]
    unnamed x17 -> x2, waiting for transfers between devices: 260 us -> 131 us
    all_gather x4 -> x0, waiting for transfers between devices: 116 us -> none  [the longest x1 36.5 us: body(): rows_all = lax.all_gather(tokens, 'tp', axis=0, tiled=True)]
    ppermute x0 -> x84, starting transfers between devices: none -> 51.8 us  [swap(): return lax.ppermute(value, axis, [(i, i ^ bit) for i in range(count)])]
    another operation x7 -> x0, local copies, waits for them, and re-layouts: 25.1 us -> none  [attend_back(): return jnp.stack([d_query, d_key, d_value]).astype(jnp.bfloat16)]
  transfers between devices with their start and end apart: 13 -> 85, of which waited for: 12 -> 39; matrix products, arithmetic and copies ran while one was open for 16% -> 4% of each run, Pallas kernels for 0% -> 18%
where the time goes in v1:
time: 604 us; the launch traced here: 594 us
  waiting for transfers between devices  312 us (52%)
  Pallas kernels  150 us (25%)
  starting transfers between devices  51.9 us (9%)
  local copies, waits for them, and re-layouts  48.9 us (8%)
  other arithmetic  16.1 us (3%)
  between operations  15.4 us (3%)
    ppermute x84, waiting for transfers between devices, swap(): return lax.ppermute(value, axis, [(i, i ^ bit) for i in range(count)])  181 us
    pallas_call x17, Pallas kernels, call(): pl.pallas_call(kernel, out_shape=out_shape, in_specs=specs, out_specs=[pl...  150 us
    unnamed x2, waiting for transfers between devices  131 us
    ppermute x84, starting transfers between devices, swap(): return lax.ppermute(value, axis, [(i, i ^ bit) for i in range(count)])  51.8 us
    unnamed x216, local copies, waits for them, and re-layouts  42.3 us
    convert_element_type x22, other arithmetic, add(): return total.astype(BF)  12.9 us
  transfers between devices with their start and end apart: 85, of which 39 were waited for; matrix products, arithmetic and copies ran while one was open for 4% of the time, Pallas kernels for 18%

profile of v1, /device:TPU:0, one launch (start us, length us, event | category | flops | bytes accessed | tf_op | source)
XLA Modules:
  0.0 594.4 jit_solution(4501923633245302121)
XLA Ops:
  8.4 3.0 collective-permute-start.2
  11.4 2.2 dynamic-slice_bitcast_fusion.2
  14.4 4.2 collective-permute-done.2.refs_4_.refs_6_
  18.6 2.0 collective-permute-start.3
  23.2 2.4 collective-permute-done.3.refs_4_.refs_11_
  31.6 3.8 collective-permute-done.refs_3_.refs_5_
  37.7 2.0 collective-permute-start.1
  39.7 18.2 %collective-permute-done.12.refs_1_.refs_3_ = bf16[1024,512]{1,0:T(8,128)(2,1)} collective-permute-done((bf16[1024,512]{1,0:T(8,128)(2,1)S(1)}, bf16[1024,512]{1,0:T(8,128)(2,1)}, u32[]{:S(2)}, u32[]{:S(2)}) %collective-permute-start.12) | collective-permute-done | bytes 1048608 | tf_op jit(solution)/shard_map/ppermute | solution.py:267
  58.0 21.6 %collective-permute-done.14.refs_2_.refs_4_ = bf16[512,1024]{1,0:T(8,128)(2,1)} collective-permute-done((bf16[512,1024]{1,0:T(8,128)(2,1)S(1)}, bf16[512,1024]{1,0:T(8,128)(2,1)}, u32[]{:S(2)}, u32[]{:S(2)}) %collective-permute-start.14) | collective-permute-done | bytes 1048608 | tf_op jit(solution)/shard_map/ppermute | solution.py:267
  85.6 20.4 %collective-permute-done.13.refs_1_.refs_7_ = bf16[1024,512]{1,0:T(8,128)(2,1)} collective-permute-done((bf16[1024,512]{1,0:T(8,128)(2,1)}, bf16[1024,512]{1,0:T(8,128)(2,1)}, u32[]{:S(2)}, u32[]{:S(2)}) %collective-permute-start.13) | collective-permute-done | bytes 1048608 | tf_op jit(solution)/shard_map/ppermute | solution.py:267
  106.0 20.7 %collective-permute-done.15.refs_2_.refs_8_ = bf16[512,1024]{1,0:T(8,128)(2,1)} collective-permute-done((bf16[512,1024]{1,0:T(8,128)(2,1)}, bf16[512,1024]{1,0:T(8,128)(2,1)}, u32[]{:S(2)}, u32[]{:S(2)}) %collective-permute-start.15) | collective-permute-done | bytes 1048608 | tf_op jit(solution)/shard_map/ppermute | solution.py:267
  130.4 6.5 %attn_fwd0.1 = (bf16[512,384]{1,0:T(8,128)(2,1)S(1)}, bf16[512,128]{1,0:T(8,128)(2,1)S(1)}, f32[2,512]{1,0:T(2,128)S(1)}, bf16[512,384]{1,0:T(8,128)(2,1)S(1)}, ...) custom-call(s32[8]{0:T(128)S(1)} %shift-right-arithmetic_add_fusion.pos_ref, ...), custom_call_target="tpu_custom_call" | custom-call | tf_op jit(solution)/shard_map/attn_fwd0/pallas_call | solution.py:34
  139.1 7.4 %attn_fwd1.1 = (bf16[512,384]{1,0:T(8,128)(2,1)S(1)}, bf16[512,128]{1,0:T(8,128)(2,1)S(1)}, f32[2,512]{1,0:T(2,128)S(1)}, bf16[512,384]{1,0:T(8,128)(2,1)S(1)}, ...) custom-call(s32[8]{0:T(128)S(1)} %shift-right-arithmetic_add_fusion.pos_ref, ...), custom_call_target="tpu_custom_call" | custom-call | tf_op jit(solution)/shard_map/attn_fwd1/pallas_call | solution.py:34
  150.0 7.7 %attn_fwd2.1 = (bf16[512,384]{1,0:T(8,128)(2,1)S(1)}, bf16[512,128]{1,0:T(8,128)(2,1)S(1)}, f32[2,512]{1,0:T(2,128)S(1)}, bf16[512,384]{1,0:T(8,128)(2,1)S(1)}, ...) custom-call(s32[8]{0:T(128)S(1)} %shift-right-arithmetic_add_fusion.pos_ref, ...), custom_call_target="tpu_custom_call" | custom-call | tf_op jit(solution)/shard_map/attn_fwd2/pallas_call | solution.py:34
  158.4 8.7 %attn_fwd3.1 = (bf16[512,384]{1,0:T(8,128)(2,1)S(1)}, bf16[512,128]{1,0:T(8,128)(2,1)S(1)}, f32[2,512]{1,0:T(2,128)S(1)}, bf16[512,384]{1,0:T(8,128)(2,1)S(1)}, ...) custom-call(s32[8]{0:T(128)S(1)} %shift-right-arithmetic_add_fusion., ...), custom_call_target="tpu_custom_call" | custom-call | tf_op jit(solution)/shard_map/attn_fwd3/pallas_call | solution.py:34
  168.5 6.4 %ffn_fwd0.1 = (bf16[512,512]{1,0:T(8,128)(2,1)S(1)}, f32[512,512]{1,0:T(8,128)S(1)}, bf16[512,512]{1,0:T(8,128)(2,1)S(1)}, f32[512,512]{1,0:T(8,128)S(1)}, f32[512,1024]{1,0:T(8,128)}) custom-call(s32[8]{0:T(128)S(1)} %shift-right-arithmetic_add_fusion.pos_ref, bf16[512,1024]{1,0:T(8,128)(2,1)} %get-tuple-element.126.refs_0_, bf16[1024,512]{1,0:T(8,128)(2,1)} %copy-done.82, ...), custom_call_target="tpu_custom_call" | custom-call | tf_op jit(solution)/shard_map/ffn_fwd0/pallas_call | solution.py:34
  176.9 7.1 %ffn_fwd1.1 = (bf16[512,512]{1,0:T(8,128)(2,1)S(1)}, f32[512,512]{1,0:T(8,128)S(1)}, bf16[512,512]{1,0:T(8,128)(2,1)S(1)}, f32[512,512]{1,0:T(8,128)S(1)}, f32[512,1024]{1,0:T(8,128)}) custom-call(s32[8]{0:T(128)S(1)} %shift-right-arithmetic_add_fusion.pos_ref, bf16[512,1024]{1,0:T(8,128)(2,1)} %get-tuple-element.126.refs_0_, bf16[1024,512]{1,0:T(8,128)(2,1)} %copy-done.84, ...), custom_call_target="tpu_custom_call" | custom-call | tf_op jit(solution)/shard_map/ffn_fwd1/pallas_call | solution.py:34
  186.0 7.3 %ffn_fwd2.1 = (bf16[512,512]{1,0:T(8,128)(2,1)S(1)}, f32[512,512]{1,0:T(8,128)S(1)}, bf16[512,512]{1,0:T(8,128)(2,1)S(1)}, f32[512,512]{1,0:T(8,128)S(1)}, f32[512,1024]{1,0:T(8,128)}) custom-call(s32[8]{0:T(128)S(1)} %shift-right-arithmetic_add_fusion.pos_ref, bf16[512,1024]{1,0:T(8,128)(2,1)} %get-tuple-element.126.refs_0_, ...), custom_call_target="tpu_custom_call" | custom-call | tf_op jit(solution)/shard_map/ffn_fwd2/pallas_call | solution.py:34
  195.3 10.3 %ffn_fwd3.1 = (bf16[512,512]{1,0:T(8,128)(2,1)S(1)}, f32[512,512]{1,0:T(8,128)S(1)}, bf16[512,512]{1,0:T(8,128)(2,1)S(1)}, f32[512,512]{1,0:T(8,128)S(1)}, bf16[...) custom-call(s32[8]{0:T(128)S(1)} %shift-right-arithmetic_add_fusion., ...), custom_call_target="tpu_custom_call" | custom-call | tf_op jit(solution)/shard_map/ffn_fwd3/pallas_call | solution.py:34
  207.6 10.1 %ffn_bwd3.1 = (bf16[1024,512]{1,0:T(8,128)(2,1)}, bf16[512,512]{1,0:T(8,128)(2,1)S(1)}, bf16[512,512]{1,0:T(8,128)(2,1)S(1)}, bf16[1024,512]{1,0:T(8,128)(2,1)},...) custom-call(s32[8]{0:T(128)S(1)} %shift-right-arithmetic_add_fusion.pos_ref, ...), custom_call_target="tpu_custom_call" | custom-call | tf_op jit(solution)/shard_map/ffn_bwd3/pallas_call | solution.py:34
  220.2 2.1 collective-permute-done.26.refs_14_
  226.1 11.1 %ffn_bwd2.1 = (bf16[1024,512]{1,0:T(8,128)(2,1)}, bf16[512,512]{1,0:T(8,128)(2,1)S(1)}, bf16[512,512]{1,0:T(8,128)(2,1)}, bf16[1024,512]{1,0:T(8,128)(2,1)}, bf1...) custom-call(s32[8]{0:T(128)S(1)} %shift-right-arithmetic_add_fusion.pos_ref, ...), custom_call_target="tpu_custom_call" | custom-call | tf_op jit(solution)/shard_map/ffn_bwd2/pallas_call | solution.py:34
  237.2 10.4 %ffn_bwd1.1 = (bf16[1024,512]{1,0:T(8,128)(2,1)}, bf16[512,512]{1,0:T(8,128)(2,1)S(1)}, bf16[512,512]{1,0:T(8,128)(2,1)S(1)}, bf16[1024,512]{1,0:T(8,128)(2,1)},...) custom-call(s32[8]{0:T(128)S(1)} %shift-right-arithmetic_add_fusion.pos_ref, ...), custom_call_target="tpu_custom_call" | custom-call | tf_op jit(solution)/shard_map/ffn_bwd1/pallas_call | solution.py:34
  258.8 13.5 %ffn_bwd0.1 = (bf16[1024,512]{1,0:T(8,128)(2,1)}, bf16[512,512]{1,0:T(8,128)(2,1)S(1)}, bf16[512,512]{1,0:T(8,128)(2,1)}, bf16[1024,512]{1,0:T(8,128)(2,1)}, bf1...) custom-call(s32[8]{0:T(128)S(1)} %shift-right-arithmetic_add_fusion., ...), custom_call_target="tpu_custom_call" | custom-call | tf_op jit(solution)/shard_map/ffn_bwd0/pallas_call | solution.py:34
  272.3 10.8 %attn_bwd3.1 = (bf16[1024,256]{1,0:T(8,128)(2,1)S(1)}, bf16[512,256]{1,0:T(8,128)(2,1)}, bf16[512,256]{1,0:T(8,128)(2,1)S(1)}, bf16[1024,256]{1,0:T(8,128)(2,1)S...) custom-call(bf16[512,1024]{1,0:T(8,128)(2,1)} %get-tuple-element.168.refs_0_, ...), custom_call_target="tpu_custom_call" | custom-call | tf_op jit(solution)/shard_map/attn_bwd3/pallas_call | solution.py:34
  289.0 2.0 add_convert_fusion.7
  295.7 2.0 add_convert_fusion.9
  301.9 2.1 add_convert_fusion.4
  304.0 131.3 %reduce-scatter.4.cloned.1.call-done = f32[32,4]{1,0:T(8,128)} async-done(((f32[1024,4]{1,0:T(8,128)}), f32[32,4]{1,0:T(8,128)}) %reduce-scatter.4.cloned.1.call-update) | async-done | bytes 528
  442.1 11.0 %attn_bwd2.1 = (bf16[1024,256]{1,0:T(8,128)(2,1)}, bf16[512,256]{1,0:T(8,128)(2,1)S(1)}, bf16[512,256]{1,0:T(8,128)(2,1)S(1)}, bf16[1024,256]{1,0:T(8,128)(2,1)}...) custom-call(bf16[512,1024]{1,0:T(8,128)(2,1)} %get-tuple-element.168.refs_0_, ...), custom_call_target="tpu_custom_call" | custom-call | tf_op jit(solution)/shard_map/attn_bwd2/pallas_call | solution.py:34
  453.2 9.6 %attn_bwd1.1 = (bf16[1024,256]{1,0:T(8,128)(2,1)S(1)}, bf16[512,256]{1,0:T(8,128)(2,1)S(1)}, bf16[512,256]{1,0:T(8,128)(2,1)S(1)}, bf16[1024,256]{1,0:T(8,128)(2...) custom-call(bf16[512,1024]{1,0:T(8,128)(2,1)} %get-tuple-element.168.refs_0_, ...), custom_call_target="tpu_custom_call" | custom-call | tf_op jit(solution)/shard_map/attn_bwd1/pallas_call | solution.py:34
  466.6 5.5 collective-permute-done.78
  475.9 5.4 collective-permute-done.69
  483.3 3.1 collective-permute-done.79
  489.0 5.5 collective-permute-done.57
  494.6 8.0 %collective-permute-done.75 = bf16[128,512]{1,0:T(8,128)(2,1)S(1)} collective-permute-done((bf16[128,512]{1,0:T(8,128)(2,1)S(1)}, bf16[128,512]{1,0:T(8,128)(2,1)S(1)}, u32[]{:S(2)}, u32[]{:S(2)}) %collective-permute-start.75) | collective-permute-done | bytes 131104 | tf_op jit(solution)/shard_map/ppermute | solution.py:267
  504.3 4.6 collective-permute-done.70
  509.1 7.5 %collective-permute-done.80 = bf16[128,512]{1,0:T(8,128)(2,1)S(1)} collective-permute-done((bf16[128,512]{1,0:T(8,128)(2,1)S(1)}, bf16[128,512]{1,0:T(8,128)(2,1)S(1)}, u32[]{:S(2)}, u32[]{:S(2)}) %collective-permute-start.80) | collective-permute-done | bytes 131104 | tf_op jit(solution)/shard_map/ppermute | solution.py:267
  521.6 10.9 %attn_bwd0.1 = (bf16[1024,256]{1,0:T(8,128)(2,1)}, bf16[512,256]{1,0:T(8,128)(2,1)S(1)}, bf16[512,256]{1,0:T(8,128)(2,1)S(1)}, bf16[1024,256]{1,0:T(8,128)(2,1)}...) custom-call(bf16[512,1024]{1,0:T(8,128)(2,1)} %get-tuple-element.168.refs_0_, ...), custom_call_target="tpu_custom_call" | custom-call | tf_op jit(solution)/shard_map/attn_bwd0/pallas_call | solution.py:34
  536.1 12.2 %collective-permute-done.63 = bf16[512,256]{1,0:T(8,128)(2,1)S(1)} collective-permute-done((bf16[512,256]{1,0:T(8,128)(2,1)S(1)}, bf16[512,256]{1,0:T(8,128)(2,1)S(1)}, u32[]{:S(2)}, u32[]{:S(2)}) %collective-permute-start.63) | collective-permute-done | bytes 262176 | tf_op jit(solution)/shard_map/ppermute | solution.py:267
  550.1 2.3 collective-permute-done.58
  552.5 2.1 collective-permute-start.59
  554.8 2.3 collective-permute-start.53
  557.2 1.9 collective-permute-done.82
  560.1 4.2 collective-permute-done.64
  564.5 2.8 collective-permute-done.59
  576.0 4.6 collective-permute-done.54
  581.0 5.5 collective-permute-done.55
  (423 shorter events, 112.9 us)
Async XLA Ops:
  7.2 428.2 %reduce-scatter.4.cloned.1.call-start = ((), (), s32[]{:S(2)}) async-start(), calls=%async_computation.1 | async-start | bytes 540672
  8.4 10.3 %collective-permute-start.2 = (bf16[128,1024]{1,0:T(8,128)(2,1)S(1)}, bf16[128,1024]{1,0:T(8,128)(2,1)}, u32[]{:S(2)}, u32[]{:S(2)}) collective-permute-start(bf16[128,1024]{1,0:T(8,128)(2,1)S(1)} %get-tuple-element.275.refs_4_.refs_6_), channel_id=1, source_target_pairs={{0,2},{1,3},{2,0},{3,1},{4,6},{5,7},{6,4},{7,5},{8,10},{9,11},{10,... | collective-permute-start | bytes 786440 | tf_op jit(solution)/shard_map/ppermute | solution.py:267
  13.7 21.6 %collective-permute-start = (bf16[1024,384]{1,0:T(8,128)(2,1)S(1)}, bf16[1024,384]{1,0:T(8,128)(2,1)S(1)}, u32[]{:S(2)}, u32[]{:S(2)}) collective-permute-start(bf16[1024,384]{1,0:T(8,128)(2,1)S(1)} %pad_maximum_fusion.refs_3_.refs_5_), channel_id=1, source_target_pairs={{0,2},{1,3},{2,0},{3,1},{4,6},{5,7},{6,4},{7,5},{8,10},{9,11},{10,... | collective-permute-start | bytes 2359304 | tf_op jit(solution)/shard_map/ppermute | solution.py:267
  20.7 14.7 %collective-permute-start.8 = (bf16[1024,384]{1,0:T(8,128)(2,1)S(1)}, bf16[1024,384]{1,0:T(8,128)(2,1)S(1)}, u32[]{:S(2)}, u32[]{:S(2)}) collective-permute-start(bf16[1024,384]{1,0:T(8,128)(2,1)S(1)} %pad_maximum_fusion.refs_3_.refs_5_), channel_id=1, source_target_pairs={{0,1},{1,0},{2,3},{3,2},{4,5},{5,4},{6,7},{7,6},{8,9},{9,8},{10,11... | collective-permute-start | bytes 2359304 | tf_op jit(solution)/shard_map/ppermute | solution.py:267
  23.1 13.7 %collective-permute-start.10 = (bf16[1024,384]{1,0:T(8,128)(2,1)S(1)}, bf16[1024,384]{1,0:T(8,128)(2,1)S(1)}, u32[]{:S(2)}, u32[]{:S(2)}) collective-permute-start(bf16[1024,384]{1,0:T(8,128)(2,1)S(1)} %pad_maximum_fusion.1.refs_5_.refs_10_), channel_id=1, source_target_pairs={{0,1},{1,0},{2,3},{3,2},{4,5},{5,4},{6,7},{7,6},{8,9},{9,8},{10,11... | collective-permute-start | bytes 2359304 | tf_op jit(solution)/shard_map/ppermute | solution.py:267
  27.3 30.6 %collective-permute-start.12 = (bf16[1024,512]{1,0:T(8,128)(2,1)S(1)}, bf16[1024,512]{1,0:T(8,128)(2,1)}, u32[]{:S(2)}, u32[]{:S(2)}) collective-permute-start(bf16[1024,512]{1,0:T(8,128)(2,1)S(1)} %get-tuple-element.265.refs_1_.refs_3_), channel_id=1, source_target_pairs={{0,2},{1,3},{2,0},{3,1},{4,6},{5,7},{6,4},{7,5},{8,10},{9,11},{10,... | collective-permute-start | bytes 3145736 | tf_op jit(solution)/shard_map/ppermute | solution.py:267
  31.1 48.5 %collective-permute-start.14 = (bf16[512,1024]{1,0:T(8,128)(2,1)S(1)}, bf16[512,1024]{1,0:T(8,128)(2,1)}, u32[]{:S(2)}, u32[]{:S(2)}) collective-permute-start(bf16[512,1024]{1,0:T(8,128)(2,1)S(1)} %get-tuple-element.263.refs_2_.refs_4_), channel_id=1, source_target_pairs={{0,2},{1,3},{2,0},{3,1},{4,6},{5,7},{6,4},{7,5},{8,10},{9,11},{10,... | collective-permute-start | bytes 3145736 | tf_op jit(solution)/shard_map/ppermute | solution.py:267
  35.4 45.9 %collective-permute-start.20 = (bf16[1024,512]{1,0:T(8,128)(2,1)S(1)}, bf16[1024,512]{1,0:T(8,128)(2,1)S(1)}, u32[]{:S(2)}, u32[]{:S(2)}) collective-permute-start(bf16[1024,512]{1,0:T(8,128)(2,1)S(1)} %get-tuple-element.265.refs_1_.refs_3_), channel_id=1, source_target_pairs={{0,1},{1,0},{2,3},{3,2},{4,5},{5,4},{6,7},{7,6},{8,9},{9,8},{10,11... | collective-permute-start | bytes 3145736 | tf_op jit(solution)/shard_map/ppermute | solution.py:267
  36.3 46.0 %collective-permute-start.21 = (bf16[512,1024]{1,0:T(8,128)(2,1)S(1)}, bf16[512,1024]{1,0:T(8,128)(2,1)}, u32[]{:S(2)}, u32[]{:S(2)}) collective-permute-start(bf16[512,1024]{1,0:T(8,128)(2,1)S(1)} %get-tuple-element.263.refs_2_.refs_4_), channel_id=1, source_target_pairs={{0,1},{1,0},{2,3},{3,2},{4,5},{5,4},{6,7},{7,6},{8,9},{9,8},{10,11... | collective-permute-start | bytes 3145736 | tf_op jit(solution)/shard_map/ppermute | solution.py:267
  37.7 44.6 %collective-permute-start.1 = (bf16[1024,384]{1,0:T(8,128)(2,1)S(1)}, bf16[1024,384]{1,0:T(8,128)(2,1)S(1)}, u32[]{:S(2)}, u32[]{:S(2)}) collective-permute-start(bf16[1024,384]{1,0:T(8,128)(2,1)S(1)} %collective-permute-done.refs_3_.refs_5_), channel_id=1, source_target_pairs={{0,4},{4,0},{8,12},{12,8},{16,20},{20,16},{24,28},{28,24},{1,5},{5... | collective-permute-start | bytes 2359304 | tf_op jit(solution)/shard_map/ppermute | solution.py:267
  58.0 24.9 %collective-permute-start.22 = (bf16[1024,512]{1,0:T(8,128)(2,1)S(1)}, bf16[1024,512]{1,0:T(8,128)(2,1)S(1)}, u32[]{:S(2)}, u32[]{:S(2)}) collective-permute-start(bf16[1024,512]{1,0:T(8,128)(2,1)S(1)} %get-tuple-element.264.refs_3_.refs_7_), channel_id=1, source_target_pairs={{0,1},{1,0},{2,3},{3,2},{4,5},{5,4},{6,7},{7,6},{8,9},{9,8},{10,11... | collective-permute-start | bytes 3145736 | tf_op jit(solution)/shard_map/ppermute | solution.py:267
  79.6 26.4 %collective-permute-start.13 = (bf16[1024,512]{1,0:T(8,128)(2,1)}, bf16[1024,512]{1,0:T(8,128)(2,1)}, u32[]{:S(2)}, u32[]{:S(2)}) collective-permute-start(bf16[1024,512]{1,0:T(8,128)(2,1)} %collective-permute-done.12.refs_1_.refs_3_), channel_id=1, source_target_pairs={{0,4},{4,0},{8,12},{12,8},{16,20},{20,16},{24,28},{28,24},{1,5},{5... | collective-permute-start | bytes 3145736 | tf_op jit(solution)/shard_map/ppermute | solution.py:267
  81.3 45.4 %collective-permute-start.15 = (bf16[512,1024]{1,0:T(8,128)(2,1)}, bf16[512,1024]{1,0:T(8,128)(2,1)}, u32[]{:S(2)}, u32[]{:S(2)}) collective-permute-start(bf16[512,1024]{1,0:T(8,128)(2,1)} %collective-permute-done.14.refs_2_.refs_4_), channel_id=1, source_target_pairs={{0,4},{4,0},{8,12},{12,8},{16,20},{20,16},{24,28},{28,24},{1,5},{5... | collective-permute-start | bytes 3145736 | tf_op jit(solution)/shard_map/ppermute | solution.py:267
  82.3 44.4 %collective-permute-start.4 = (bf16[1024,384]{1,0:T(8,128)(2,1)S(1)}, bf16[1024,384]{1,0:T(8,128)(2,1)S(1)}, u32[]{:S(2)}, u32[]{:S(2)}) collective-permute-start(bf16[1024,384]{1,0:T(8,128)(2,1)S(1)} %collective-permute-done.1.refs_3_.refs_10_), channel_id=1, source_target_pairs={{0,1},{1,0},{2,3},{3,2},{4,5},{5,4},{6,7},{7,6},{8,9},{9,8},{10,11... | collective-permute-start | bytes 2359304 | tf_op jit(solution)/shard_map/ppermute | solution.py:267
  82.8 94.0 %collective-permute-start.23 = (bf16[512,1024]{1,0:T(8,128)(2,1)}, bf16[512,1024]{1,0:T(8,128)(2,1)}, u32[]{:S(2)}, u32[]{:S(2)}) collective-permute-start(bf16[512,1024]{1,0:T(8,128)(2,1)} %get-tuple-element.262.refs_4_.refs_8_), channel_id=1, source_target_pairs={{0,1},{1,0},{2,3},{3,2},{4,5},{5,4},{6,7},{7,6},{8,9},{9,8},{10,11... | collective-permute-start | bytes 3145736 | tf_op jit(solution)/shard_map/ppermute | solution.py:267
  85.5 100.4 %collective-permute-start.18 = (bf16[1024,512]{1,0:T(8,128)(2,1)}, bf16[1024,512]{1,0:T(8,128)(2,1)}, u32[]{:S(2)}, u32[]{:S(2)}) collective-permute-start(bf16[1024,512]{1,0:T(8,128)(2,1)} %collective-permute-done.12.refs_1_.refs_3_), channel_id=1, source_target_pairs={{0,1},{1,0},{2,3},{3,2},{4,5},{5,4},{6,7},{7,6},{8,9},{9,8},{10,11... | collective-permute-start | bytes 3145736 | tf_op jit(solution)/shard_map/ppermute | solution.py:267
  106.0 79.9 %collective-permute-start.19 = (bf16[512,1024]{1,0:T(8,128)(2,1)}, bf16[512,1024]{1,0:T(8,128)(2,1)}, u32[]{:S(2)}, u32[]{:S(2)}) collective-permute-start(bf16[512,1024]{1,0:T(8,128)(2,1)} %collective-permute-done.14.refs_2_.refs_4_), channel_id=1, source_target_pairs={{0,1},{1,0},{2,3},{3,2},{4,5},{5,4},{6,7},{7,6},{8,9},{9,8},{10,11... | collective-permute-start | bytes 3145736 | tf_op jit(solution)/shard_map/ppermute | solution.py:267
  126.7 68.5 %collective-permute-start.16 = (bf16[1024,512]{1,0:T(8,128)(2,1)}, bf16[1024,512]{1,0:T(8,128)(2,1)}, u32[]{:S(2)}, u32[]{:S(2)}) collective-permute-start(bf16[1024,512]{1,0:T(8,128)(2,1)} %collective-permute-done.13.refs_1_.refs_7_), channel_id=1, source_target_pairs={{0,1},{1,0},{2,3},{3,2},{4,5},{5,4},{6,7},{7,6},{8,9},{9,8},{10,11... | collective-permute-start | bytes 3145736 | tf_op jit(solution)/shard_map/ppermute | solution.py:267
  127.7 67.6 %collective-permute-start.17 = (bf16[512,1024]{1,0:T(8,128)(2,1)}, bf16[512,1024]{1,0:T(8,128)(2,1)}, u32[]{:S(2)}, u32[]{:S(2)}) collective-permute-start(bf16[512,1024]{1,0:T(8,128)(2,1)} %collective-permute-done.15.refs_2_.refs_8_), channel_id=1, source_target_pairs={{0,1},{1,0},{2,3},{3,2},{4,5},{5,4},{6,7},{7,6},{8,9},{9,8},{10,11... | collective-permute-start | bytes 3145736 | tf_op jit(solution)/shard_map/ppermute | solution.py:267
  251.0 36.9 %collective-permute-start.77 = (bf16[1024,512]{1,0:T(8,128)(2,1)}, bf16[1024,512]{1,0:T(8,128)(2,1)}, u32[]{:S(2)}, u32[]{:S(2)}) collective-permute-start(bf16[1024,512]{1,0:T(8,128)(2,1)} %get-tuple-element.234), channel_id=1, source_target_pairs={{0,2},{1,3},{2,0},{3,1},{4,6},{5,7},{6,4},{7,5},{8,10},{9,11},{10,... | collective-permute-start | bytes 3145736 | tf_op jit(solution)/shard_map/ppermute | solution.py:267
  252.5 34.9 %collective-permute-start.72 = (bf16[512,512]{1,0:T(8,128)(2,1)}, bf16[512,512]{1,0:T(8,128)(2,1)}, u32[]{:S(2)}, u32[]{:S(2)}) collective-permute-start(bf16[512,512]{1,0:T(8,128)(2,1)} %get-tuple-element.230), channel_id=1, source_target_pairs={{0,4},{4,0},{8,12},{12,8},{16,20},{20,16},{24,28},{28,24},{1,5},{5... | collective-permute-start | bytes 1572872 | tf_op jit(solution)/shard_map/ppermute | solution.py:267
  254.0 33.3 %collective-permute-start.67 = (bf16[512,512]{1,0:T(8,128)(2,1)S(1)}, bf16[512,512]{1,0:T(8,128)(2,1)}, u32[]{:S(2)}, u32[]{:S(2)}) collective-permute-start(bf16[512,512]{1,0:T(8,128)(2,1)S(1)} %get-tuple-element.226), channel_id=1, source_target_pairs={{0,4},{4,0},{8,12},{12,8},{16,20},{20,16},{24,28},{28,24},{1,5},{5... | collective-permute-start | bytes 1572872 | tf_op jit(solution)/shard_map/ppermute | solution.py:267
  286.8 12.0 %collective-permute-start.36 = (bf16[1024,256]{1,0:T(8,128)(2,1)}, bf16[1024,256]{1,0:T(8,128)(2,1)}, u32[]{:S(2)}, u32[]{:S(2)}) collective-permute-start(bf16[1024,256]{1,0:T(8,128)(2,1)} %copy-done.77), channel_id=1, source_target_pairs={{0,1},{1,0},{2,3},{3,2},{4,5},{5,4},{6,7},{7,6},{8,9},{9,8},{10,11... | collective-permute-start | bytes 1572872 | tf_op jit(solution)/shard_map/ppermute | solution.py:267
  287.3 13.1 %collective-permute-start.39 = (bf16[1024,256]{1,0:T(8,128)(2,1)}, bf16[1024,256]{1,0:T(8,128)(2,1)}, u32[]{:S(2)}, u32[]{:S(2)}) collective-permute-start(bf16[1024,256]{1,0:T(8,128)(2,1)} %copy-done.76), channel_id=1, source_target_pairs={{0,1},{1,0},{2,3},{3,2},{4,5},{5,4},{6,7},{7,6},{8,9},{9,8},{10,11... | collective-permute-start | bytes 1572872 | tf_op jit(solution)/shard_map/ppermute | solution.py:267
  291.7 174.8 %collective-permute-start.76 = (bf16[1024,512]{1,0:T(8,128)(2,1)}, bf16[1024,512]{1,0:T(8,128)(2,1)}, u32[]{:S(2)}, u32[]{:S(2)}) collective-permute-start(bf16[1024,512]{1,0:T(8,128)(2,1)} %get-tuple-element.232), channel_id=1, source_target_pairs={{0,2},{1,3},{2,0},{3,1},{4,6},{5,7},{6,4},{7,5},{8,10},{9,11},{10,... | collective-permute-start | bytes 3145736 | tf_op jit(solution)/shard_map/ppermute | solution.py:267
  293.9 168.8 %collective-permute-start.73 = (bf16[512,512]{1,0:T(8,128)(2,1)}, bf16[512,512]{1,0:T(8,128)(2,1)}, u32[]{:S(2)}, u32[]{:S(2)}) collective-permute-start(bf16[512,512]{1,0:T(8,128)(2,1)} %add_convert_fusion.7), channel_id=1, source_target_pairs={{0,2},{1,3},{2,0},{3,1},{4,6},{5,7},{6,4},{7,5},{8,10},{9,11},{10,... | collective-permute-start | bytes 1572872 | tf_op jit(solution)/shard_map/ppermute | solution.py:267
  295.2 167.7 %collective-permute-start.71 = (bf16[512,512]{1,0:T(8,128)(2,1)}, bf16[512,512]{1,0:T(8,128)(2,1)}, u32[]{:S(2)}, u32[]{:S(2)}) collective-permute-start(bf16[512,512]{1,0:T(8,128)(2,1)} %get-tuple-element.228), channel_id=1, source_target_pairs={{0,4},{4,0},{8,12},{12,8},{16,20},{20,16},{24,28},{28,24},{1,5},{5... | collective-permute-start | bytes 1572872 | tf_op jit(solution)/shard_map/ppermute | solution.py:267
  298.9 165.5 %collective-permute-start.68 = (bf16[512,512]{1,0:T(8,128)(2,1)}, bf16[512,512]{1,0:T(8,128)(2,1)}, u32[]{:S(2)}, u32[]{:S(2)}) collective-permute-start(bf16[512,512]{1,0:T(8,128)(2,1)} %add_convert_fusion.9), channel_id=1, source_target_pairs={{0,2},{1,3},{2,0},{3,1},{4,6},{5,7},{6,4},{7,5},{8,10},{9,11},{10,... | collective-permute-start | bytes 1572872 | tf_op jit(solution)/shard_map/ppermute | solution.py:267
  300.4 164.5 %collective-permute-start.66 = (bf16[512,512]{1,0:T(8,128)(2,1)}, bf16[512,512]{1,0:T(8,128)(2,1)}, u32[]{:S(2)}, u32[]{:S(2)}) collective-permute-start(bf16[512,512]{1,0:T(8,128)(2,1)} %copy-done.75), channel_id=1, source_target_pairs={{0,4},{4,0},{8,12},{12,8},{16,20},{20,16},{24,28},{28,24},{1,5},{5... | collective-permute-start | bytes 1572872 | tf_op jit(solution)/shard_map/ppermute | solution.py:267
  462.9 56.7 %collective-permute-start.42 = (bf16[1024,256]{1,0:T(8,128)(2,1)S(1)}, bf16[1024,256]{1,0:T(8,128)(2,1)S(1)}, u32[]{:S(2)}, u32[]{:S(2)}) collective-permute-start(bf16[1024,256]{1,0:T(8,128)(2,1)S(1)} %get-tuple-element.204), channel_id=1, source_target_pairs={{0,1},{1,0},{2,3},{3,2},{4,5},{5,4},{6,7},{7,6},{8,9},{9,8},{10,11... | collective-permute-start | bytes 1572872 | tf_op jit(solution)/shard_map/ppermute | solution.py:267
  464.4 38.2 %collective-permute-start.43 = (bf16[512,256]{1,0:T(8,128)(2,1)S(1)}, bf16[512,256]{1,0:T(8,128)(2,1)S(1)}, u32[]{:S(2)}, u32[]{:S(2)}) collective-permute-start(bf16[512,256]{1,0:T(8,128)(2,1)S(1)} %get-tuple-element.205), channel_id=1, source_target_pairs={{0,1},{1,0},{2,3},{3,2},{4,5},{5,4},{6,7},{7,6},{8,9},{9,8},{10,11... | collective-permute-start | bytes 786440 | tf_op jit(solution)/shard_map/ppermute | solution.py:267
  465.0 37.7 %collective-permute-start.44 = (bf16[512,256]{1,0:T(8,128)(2,1)S(1)}, bf16[512,256]{1,0:T(8,128)(2,1)S(1)}, u32[]{:S(2)}, u32[]{:S(2)}) collective-permute-start(bf16[512,256]{1,0:T(8,128)(2,1)S(1)} %get-tuple-element.206), channel_id=1, source_target_pairs={{0,1},{1,0},{2,3},{3,2},{4,5},{5,4},{6,7},{7,6},{8,9},{9,8},{10,11... | collective-permute-start | bytes 786440 | tf_op jit(solution)/shard_map/ppermute | solution.py:267
  475.7 10.8 %collective-permute-start.79 = (bf16[256,512]{1,0:T(8,128)(2,1)S(1)}, bf16[256,512]{1,0:T(8,128)(2,1)S(1)}, u32[]{:S(2)}, u32[]{:S(2)}) collective-permute-start(bf16[256,512]{1,0:T(8,128)(2,1)S(1)} %slice.287), channel_id=1, source_target_pairs={{0,8},{4,12},{8,0},{12,4},{16,24},{20,28},{24,16},{28,20},{1,9},{5... | collective-permute-start | bytes 786440 | tf_op jit(solution)/shard_map/ppermute | solution.py:267
  488.9 20.1 %collective-permute-start.46 = (bf16[512,256]{1,0:T(8,128)(2,1)S(1)}, bf16[512,256]{1,0:T(8,128)(2,1)S(1)}, u32[]{:S(2)}, u32[]{:S(2)}) collective-permute-start(bf16[512,256]{1,0:T(8,128)(2,1)S(1)} %get-tuple-element.208), channel_id=1, source_target_pairs={{0,1},{1,0},{2,3},{3,2},{4,5},{5,4},{6,7},{7,6},{8,9},{9,8},{10,11... | collective-permute-start | bytes 786440 | tf_op jit(solution)/shard_map/ppermute | solution.py:267
  502.6 18.1 %collective-permute-start.45 = (bf16[1024,256]{1,0:T(8,128)(2,1)S(1)}, bf16[1024,256]{1,0:T(8,128)(2,1)S(1)}, u32[]{:S(2)}, u32[]{:S(2)}) collective-permute-start(bf16[1024,256]{1,0:T(8,128)(2,1)S(1)} %get-tuple-element.207), channel_id=1, source_target_pairs={{0,1},{1,0},{2,3},{3,2},{4,5},{5,4},{6,7},{7,6},{8,9},{9,8},{10,11... | collective-permute-start | bytes 1572872 | tf_op jit(solution)/shard_map/ppermute | solution.py:267
  502.7 29.8 %collective-permute-start.81 = (bf16[512,512]{1,0:T(8,128)(2,1)S(1)}, bf16[512,512]{1,0:T(8,128)(2,1)S(1)}, u32[]{:S(2)}, u32[]{:S(2)}) collective-permute-start(bf16[512,512]{1,0:T(8,128)(2,1)S(1)} %get-tuple-element.261), channel_id=1, source_target_pairs={{0,4},{4,0},{8,12},{12,8},{16,20},{20,16},{24,28},{28,24},{1,5},{5... | collective-permute-start | bytes 1572872 | tf_op jit(solution)/shard_map/ppermute | solution.py:267
  509.0 9.7 %collective-permute-start.47 = (bf16[512,256]{1,0:T(8,128)(2,1)S(1)}, bf16[512,256]{1,0:T(8,128)(2,1)S(1)}, u32[]{:S(2)}, u32[]{:S(2)}) collective-permute-start(bf16[512,256]{1,0:T(8,128)(2,1)S(1)} %get-tuple-element.209), channel_id=1, source_target_pairs={{0,1},{1,0},{2,3},{3,2},{4,5},{5,4},{6,7},{7,6},{8,9},{9,8},{10,11... | collective-permute-start | bytes 786440 | tf_op jit(solution)/shard_map/ppermute | solution.py:267
  516.5 19.2 %collective-permute-start.49 = (bf16[1024,256]{1,0:T(8,128)(2,1)S(1)}, bf16[1024,256]{1,0:T(8,128)(2,1)S(1)}, u32[]{:S(2)}, u32[]{:S(2)}) collective-permute-start(bf16[1024,256]{1,0:T(8,128)(2,1)S(1)} %copy-done.105), channel_id=1, source_target_pairs={{0,2},{1,3},{2,0},{3,1},{4,6},{5,7},{6,4},{7,5},{8,10},{9,11},{10,... | collective-permute-start | bytes 1572872 | tf_op jit(solution)/shard_map/ppermute | solution.py:267
  518.7 36.0 %collective-permute-start.48 = (bf16[1024,256]{1,0:T(8,128)(2,1)S(1)}, bf16[1024,256]{1,0:T(8,128)(2,1)S(1)}, u32[]{:S(2)}, u32[]{:S(2)}) collective-permute-start(bf16[1024,256]{1,0:T(8,128)(2,1)S(1)} %copy-done.104), channel_id=1, source_target_pairs={{0,2},{1,3},{2,0},{3,1},{4,6},{5,7},{6,4},{7,5},{8,10},{9,11},{10,... | collective-permute-start | bytes 1572872 | tf_op jit(solution)/shard_map/ppermute | solution.py:267
  519.5 28.7 %collective-permute-start.63 = (bf16[512,256]{1,0:T(8,128)(2,1)S(1)}, bf16[512,256]{1,0:T(8,128)(2,1)S(1)}, u32[]{:S(2)}, u32[]{:S(2)}) collective-permute-start(bf16[512,256]{1,0:T(8,128)(2,1)S(1)} %add_convert_fusion.15), channel_id=1, source_target_pairs={{0,2},{1,3},{2,0},{3,1},{4,6},{5,7},{6,4},{7,5},{8,10},{9,11},{10,... | collective-permute-start | bytes 786440 | tf_op jit(solution)/shard_map/ppermute | solution.py:267
  520.8 31.7 %collective-permute-start.58 = (bf16[512,256]{1,0:T(8,128)(2,1)S(1)}, bf16[512,256]{1,0:T(8,128)(2,1)S(1)}, u32[]{:S(2)}, u32[]{:S(2)}) collective-permute-start(bf16[512,256]{1,0:T(8,128)(2,1)S(1)} %add_convert_fusion.17), channel_id=1, source_target_pairs={{0,2},{1,3},{2,0},{3,1},{4,6},{5,7},{6,4},{7,5},{8,10},{9,11},{10,... | collective-permute-start | bytes 786440 | tf_op jit(solution)/shard_map/ppermute | solution.py:267
  532.5 17.5 %collective-permute-start.61 = (bf16[512,256]{1,0:T(8,128)(2,1)S(1)}, bf16[512,256]{1,0:T(8,128)(2,1)S(1)}, u32[]{:S(2)}, u32[]{:S(2)}) collective-permute-start(bf16[512,256]{1,0:T(8,128)(2,1)S(1)} %get-tuple-element.220), channel_id=1, source_target_pairs={{0,4},{4,0},{8,12},{12,8},{16,20},{20,16},{24,28},{28,24},{1,5},{5... | collective-permute-start | bytes 786440 | tf_op jit(solution)/shard_map/ppermute | solution.py:267
  535.7 16.7 %collective-permute-start.56 = (bf16[512,256]{1,0:T(8,128)(2,1)S(1)}, bf16[512,256]{1,0:T(8,128)(2,1)S(1)}, u32[]{:S(2)}, u32[]{:S(2)}) collective-permute-start(bf16[512,256]{1,0:T(8,128)(2,1)S(1)} %get-tuple-element.216), channel_id=1, source_target_pairs={{0,4},{4,0},{8,12},{12,8},{16,20},{20,16},{24,28},{28,24},{1,5},{5... | collective-permute-start | bytes 786440 | tf_op jit(solution)/shard_map/ppermute | solution.py:267
  552.4 11.9 %collective-permute-start.64 = (bf16[256,256]{1,0:T(8,128)(2,1)S(1)}, bf16[256,256]{1,0:T(8,128)(2,1)S(1)}, u32[]{:S(2)}, u32[]{:S(2)}) collective-permute-start(bf16[256,256]{1,0:T(8,128)(2,1)S(1)} %slice.270), channel_id=1, source_target_pairs={{0,8},{4,12},{8,0},{12,4},{16,24},{20,28},{24,16},{28,20},{1,9},{5... | collective-permute-start | bytes 393224 | tf_op jit(solution)/shard_map/ppermute | solution.py:267
  552.5 14.7 %collective-permute-start.59 = (bf16[256,256]{1,0:T(8,128)(2,1)S(1)}, bf16[256,256]{1,0:T(8,128)(2,1)S(1)}, u32[]{:S(2)}, u32[]{:S(2)}) collective-permute-start(bf16[256,256]{1,0:T(8,128)(2,1)S(1)} %slice.265), channel_id=1, source_target_pairs={{0,8},{4,12},{8,0},{12,4},{16,24},{20,28},{24,16},{28,20},{1,9},{5... | collective-permute-start | bytes 393224 | tf_op jit(solution)/shard_map/ppermute | solution.py:267
  554.8 20.5 %collective-permute-start.53 = (bf16[512,256]{1,0:T(8,128)(2,1)S(1)}, bf16[512,256]{1,0:T(8,128)(2,1)S(1)}, u32[]{:S(2)}, u32[]{:S(2)}) collective-permute-start(bf16[512,256]{1,0:T(8,128)(2,1)S(1)} %get-tuple-element.273), channel_id=1, source_target_pairs={{0,4},{4,0},{8,12},{12,8},{16,20},{20,16},{24,28},{28,24},{1,5},{5... | collective-permute-start | bytes 786440 | tf_op jit(solution)/shard_map/ppermute | solution.py:267
  557.1 11.6 %collective-permute-start.51 = (bf16[256,256]{1,0:T(8,128)(2,1)S(1)}, bf16[256,256]{1,0:T(8,128)(2,1)S(1)}, u32[]{:S(2)}, u32[]{:S(2)}) collective-permute-start(bf16[256,256]{1,0:T(8,128)(2,1)S(1)} %slice.251), channel_id=1, source_target_pairs={{0,8},{4,12},{8,0},{12,4},{16,24},{20,28},{24,16},{28,20},{1,9},{5... | collective-permute-start | bytes 393224 | tf_op jit(solution)/shard_map/ppermute | solution.py:267
  559.2 12.2 %collective-permute-start.83 = (bf16[128,512]{1,0:T(8,128)(2,1)S(1)}, bf16[128,512]{1,0:T(8,128)(2,1)S(1)}, u32[]{:S(2)}, u32[]{:S(2)}) collective-permute-start(bf16[128,512]{1,0:T(8,128)(2,1)S(1)} %slice.295), channel_id=1, source_target_pairs={{0,16},{4,20},{8,24},{12,28},{16,0},{20,4},{24,8},{28,12},{1,17},{... | collective-permute-start | bytes 393224 | tf_op jit(solution)/shard_map/ppermute | solution.py:267
  (143 other events, 1825.2 us)
Sparse Core Ops, SparseCore 0:
  299.0 136.3 reduce-scatter.3

commit v2 on v1

v2 whole, which is shorter than its diff:
```python
import functools

import jax
import jax.numpy as jnp
from jax import lax
from jax.experimental import pallas as pl
from jax.experimental.pallas import tpu as pltpu
from jax.sharding import PartitionSpec as P

HDIM = 64
LANE = 128
BF = jnp.bfloat16
F32 = jnp.float32
SCALE = HDIM ** (-0.5)
MASKED = -1000000000.0
SIDE = 8


def dot(left, right):
    return jnp.dot(left, right, preferred_element_type=F32)


def dot_nt(left, right):
    return lax.dot_general(left, right, (((1,), (1,)), ((), ())), preferred_element_type=F32)


def everything(ref, scal):
    return ref


class Need:
    def __init__(self, shape, dtype, *parts):
        self.shape, self.dtype, self.parts = tuple(shape), dtype, parts


def need(array):
    return Need(array.shape, array.dtype, (array, everything, everything))


class Loads:
    def __init__(self, needs, refs, bufs, sems, scal):
        self.bufs, self.copies, self.next = bufs, [], 0
        at = 0
        for item, buf in zip(needs, bufs):
            mine = []
            for index, source, target in item.parts:
                copy = pltpu.make_async_copy(
                    source(refs[index], scal), target(buf, scal), sems.at[at]
                )
                copy.start()
                mine.append(copy)
                at += 1
            self.copies.append(mine)

    def take(self):
        self.next += 1
        return self.next - 1

    def get(self, slot):
        for copy in self.copies[slot]:
            copy.wait()
        self.copies[slot] = []
        return self.bufs[slot]

    def pop(self):
        return self.get(self.take())

    def finish(self):
        for slot in range(len(self.copies)):
            self.get(slot)


class Stores:
    def __init__(self, refs, bufs, sems):
        self.refs, self.bufs, self.sems, self.copies = refs, bufs, sems, []
        self.next = 0

    def part(self, slot, value, *where):
        self.bufs[slot][where] = value

    def send(self, slot, *where):
        source, target = self.bufs[slot], self.refs[slot]
        if where:
            source, target = source.at[where], target.at[where]
        copy = pltpu.make_async_copy(source, target, self.sems.at[self.next])
        self.next += 1
        copy.start()
        self.copies.append(copy)

    def put(self, slot, value):
        self.bufs[slot][...] = value
        self.send(slot)

    def finish(self):
        for copy in self.copies:
            copy.wait()


def call(kernel, needs, outs, scal, small, name, flops, sends=None):
    arrays, parts = [], []
    for item in needs:
        fixed = []
        for array, source, target in item.parts:
            index = next((i for i, a in enumerate(arrays) if a is array), None)
            if index is None:
                index = len(arrays)
                arrays.append(array)
            fixed.append((index, source, target))
        parts.append(Need(item.shape, item.dtype, *fixed))
    copies = sum(len(item.parts) for item in parts)
    sends = len(outs) if sends is None else sends

    def run(*refs):
        refs = list(refs)
        scal_ref = refs.pop(0)
        small_refs = [refs.pop(0) for _ in small]
        in_refs = [refs.pop(0) for _ in arrays]
        out_refs = [refs.pop(0) for _ in outs]
        in_bufs = [refs.pop(0) for _ in parts]
        out_bufs = [refs.pop(0) for _ in outs]
        in_sems, out_sems = refs
        loads = Loads(parts, in_refs, in_bufs, in_sems, scal_ref)
        stores = Stores(out_refs, out_bufs, out_sems)
        kernel(scal_ref, small_refs, loads, stores)
        loads.finish()
        stores.finish()

    moved = sum(a.size * a.dtype.itemsize for a in arrays)
    return pl.pallas_call(
        run,
        out_shape=[jax.ShapeDtypeStruct(shape, dtype) for shape, dtype in outs],
        in_specs=[pl.BlockSpec(memory_space=pltpu.SMEM)]
        + [pl.BlockSpec(memory_space=pltpu.VMEM)] * len(small)
        + [pl.BlockSpec(memory_space=pl.ANY)] * len(arrays),
        out_specs=[pl.BlockSpec(memory_space=pl.ANY)] * len(outs),
        scratch_shapes=[pltpu.VMEM(item.shape, item.dtype) for item in parts]
        + [pltpu.VMEM(shape, dtype) for shape, dtype in outs]
        + [pltpu.SemaphoreType.DMA((copies,)), pltpu.SemaphoreType.DMA((max(1, sends),))],
        compiler_params=pltpu.CompilerParams(vmem_limit_bytes=48 * 1024 * 1024),
        cost_estimate=pl.CostEstimate(flops=flops, bytes_accessed=moved, transcendentals=0),
        name=name,
    )(scal, *small, *arrays)


def store_turned(scal, buf, values):
    for block in range(values.shape[1] // LANE):
        start = pl.multiple_of(scal[block] * LANE, LANE)
        buf[pl.ds(start, LANE), :] = values[:, block * LANE : (block + 1) * LANE].T


def block_of(scal, place):
    kind, value = place
    if kind == "side":
        return lax.rem(scal[SIDE] + value, 2)
    return value


def columns(place, size, *front):
    def take(ref, scal):
        start = pl.multiple_of(block_of(scal, place) * size, size)
        return ref.at[(*front, slice(None), pl.ds(start, size))]

    return take


def lines(place, size):
    def take(ref, scal):
        start = pl.multiple_of(block_of(scal, place) * size, size)
        return ref.at[pl.ds(start, size), :]

    return take


def lanes_at(start, size):
    return lambda ref, scal: ref.at[:, pl.ds(start, size)]


def attn_needs(unit):
    if unit[0] == "half":
        return [need(unit[1])]
    _, qkv, out, _, _, place = unit
    depth, width = qkv.shape[1], out.shape[1]
    return [
        Need(
            (depth, 3 * LANE), BF,
            *[(qkv, columns(place, LANE, i), lanes_at(i * LANE, LANE)) for i in range(3)],
        ),
        Need((LANE, width), BF, (out, lines(place, LANE), everything)),
    ]


def up_need(unit, hidden):
    if unit[0] == "half":
        return need(unit[2])
    return Need((unit[3].shape[0], hidden), BF, (unit[3], columns(unit[5], hidden), everything))


def down_need(unit, hidden):
    if unit[0] == "half":
        return need(unit[3])
    return Need((hidden, unit[4].shape[1]), BF, (unit[4], lines(unit[5], hidden), everything))


def mean_of(values):
    return jnp.mean(values, axis=-1, keepdims=True)


def bias_of(seg_col, seg_row):
    return jnp.where(seg_col == seg_row, 0.0, MASKED)


def qkv_part(kind, buf):
    return buf[:, : 3 * LANE] if kind == "half" else buf[...]


def cut_kernel(scal, small, loads, stores):
    qkv, out = loads.pop(), loads.pop()
    stores.part(0, out[...].T, slice(None), slice(3 * LANE, 4 * LANE))
    stores.part(0, qkv[...], slice(None), slice(0, 3 * LANE))
    stores.send(0)


def turn_kernel(scal, small, loads, stores):
    store_turned(scal, stores.bufs[0], loads.pop()[...])
    stores.send(0)


def attn_fwd_kernel(kinds, first, last, scal, small, loads, stores):
    col_ref, row_ref = small[:2]
    tokens = loads.pop()[...]
    bias = bias_of(col_ref[...], row_ref[...])
    lane = lax.broadcasted_iota(jnp.int32, (1, LANE), 1)
    line = lax.broadcasted_iota(jnp.int32, (LANE, 1), 0)
    contexts, outs = [], []
    for number, kind in enumerate(kinds):
        weight = loads.pop()
        outs.append(loads.take() if kind == "whole" else weight)
        qkv = dot(tokens, qkv_part(kind, weight)).astype(BF)
        stores.put(number * 3, qkv)
        query, key, value = (qkv[:, i * LANE : (i + 1) * LANE] for i in range(3))
        query = query * jnp.asarray(SCALE, BF)
        value_t = value.T
        parts = []
        for head in range(2):
            mine = lane >= HDIM if head else lane < HDIM
            scores = dot_nt(jnp.where(mine, key, jnp.zeros_like(key)), query) + bias
            peak = jnp.max(scores, axis=0, keepdims=True)
            raw = jnp.exp(scores - peak)
            summed = jnp.sum(raw, axis=0, keepdims=True)
            stores.part(number * 3 + 2, peak + jnp.log(summed), pl.ds(head, 1), slice(None))
            prob = (raw * (1.0 / summed)).astype(BF)
            parts.append(dot(value_t, prob))
        stores.send(number * 3 + 2)
        context = jnp.where(line < HDIM, parts[0], parts[1]).astype(BF).T
        stores.put(number * 3 + 1, context)
        contexts.append(context)
    both = jnp.concatenate(contexts, axis=1)
    if kinds[0] == "whole":
        total = dot(both, jnp.concatenate([loads.get(slot)[...] for slot in outs], axis=0))
    else:
        total = dot_nt(both, jnp.concatenate([w[:, 3 * LANE :] for w in outs], axis=1))
    if not first:
        total = total + loads.pop()[...]
    at = len(kinds) * 3
    if not last:
        stores.put(at, total)
        return
    gain_ref, shift_ref = small[2:]
    pre = tokens.astype(F32) + total
    center = pre - mean_of(pre)
    inv = lax.rsqrt(mean_of(center * center) + 1e-12)
    hat = center * inv
    low = (hat * gain_ref[...] + shift_ref[...]).astype(BF)
    stores.put(at + 2, low)
    stores.put(at, hat)
    stores.put(at + 1, jnp.broadcast_to(inv, (hat.shape[0], LANE)))
    store_turned(scal, stores.bufs[at + 3], low)
    stores.send(at + 3)


def ffn_fwd_kernel(units, first, last, scal, small, loads, stores):
    low = loads.pop()[...]
    total = None
    for number in range(units):
        up = dot(low, loads.pop()[...])
        phi_big = 0.5 + 0.5 * lax.erf(up * (0.5 ** 0.5))
        phi_small = jnp.exp(up * up * -0.5) * 0.3989422804014327
        act = (up * phi_big).astype(BF)
        stores.put(number * 2, act)
        stores.put(number * 2 + 1, (phi_big + up * phi_small).astype(BF))
        part = dot(act, loads.pop()[...])
        total = part if total is None else total + part
    if not first:
        total = total + loads.pop()[...]
    at = units * 2
    if not last:
        stores.put(at, total)
        return
    gain1_ref, shift1_ref, gain2_ref, shift2_ref = small
    gain2 = gain2_ref[...]
    pre = loads.pop()[...] * gain1_ref[...] + shift1_ref[...] + total
    center = pre - mean_of(pre)
    inv = lax.rsqrt(mean_of(center * center) + 1e-12)
    hat = center * inv
    cot = loads.pop()[...].astype(F32)
    scaled = cot * gain2
    dpre = (scaled - mean_of(scaled) - hat * mean_of(scaled * hat)) * inv
    dffn = dpre.astype(BF)
    stores.put(at + 2, dffn)
    stores.put(at + 1, dpre)
    store_turned(scal, stores.bufs[at + 3], dffn)
    stores.send(at + 3)
    stores.put(at, (hat * gain2 + shift2_ref[...]).astype(BF))
    stores.put(at + 4, jnp.sum(cot * hat, axis=0, keepdims=True))
    stores.put(at + 5, jnp.sum(cot, axis=0, keepdims=True))


def ffn_bwd_kernel(near, has_recv, last, scal, small, loads, stores):
    dffn = loads.pop()[...]
    total = None
    ups = []
    dffn_t = low_t = None
    for unit in range(2):
        wd, slope = loads.pop(), loads.pop()
        d_up = (dot_nt(dffn, wd[...]) * slope[...].astype(F32)).astype(BF)
        if unit == 0:
            low_t = loads.pop()[...]
        up = dot(low_t, d_up)
        half = up.shape[0] // 2
        if unit == 0:
            dffn_t = loads.pop()[...]
        act = loads.pop()
        down = dot(dffn_t, act[...])
        if has_recv:
            got = loads.pop()
            down = down + got[0].astype(F32)
            up = up + got[1].astype(F32)
        down, up = down.astype(BF), up.astype(BF)
        if near:
            stores.part(0, down, unit)
            stores.send(0, unit)
            stores.part(1, up[:half], unit)
            stores.send(1, unit)
            stores.part(2, up[half:], unit)
            stores.send(2, unit)
        else:
            stores.part(0, down, unit, 0)
            stores.part(0, up, unit, 1)
            stores.send(0, unit)
        part = dot_nt(d_up, loads.pop()[...])
        total = part if total is None else total + part
    total = total + loads.pop()[...]
    at = 3 if near else 1
    if not last:
        stores.put(at, total)
        return
    hat = loads.pop()[...]
    scaled = total * small[0][...]
    inv = loads.pop()[:, :1]
    dpre = (scaled - mean_of(scaled) - hat * mean_of(scaled * hat)) * inv
    datt = dpre.astype(BF)
    stores.put(at + 1, datt)
    stores.put(at, dpre)
    store_turned(scal, stores.bufs[at + 2], datt)
    stores.send(at + 2)
    stores.put(at + 3, jnp.sum(total * hat, axis=0, keepdims=True))
    stores.put(at + 4, jnp.sum(total, axis=0, keepdims=True))


def attn_bwd_kernel(kind, near, has_recv, scal, small, loads, stores):
    bias = bias_of(small[0][...], small[1][...])
    lane = lax.broadcasted_iota(jnp.int32, (1, LANE), 1)
    line = lax.broadcasted_iota(jnp.int32, (LANE, 1), 0)
    datt = loads.pop()[...]
    weights = []
    for _ in range(2):
        weights.append((loads.take(), loads.take() if kind == "whole" else None))
    if kind == "whole":
        wo = jnp.concatenate([loads.get(slot)[...] for _, slot in weights], axis=0)
        dctx_all = dot_nt(datt, wo).astype(BF)
    else:
        wo = jnp.concatenate([loads.get(slot)[:, 3 * LANE :] for slot, _ in weights], axis=1)
        dctx_all = dot(datt, wo).astype(BF)
    grads, contexts = [], []
    for index in range(2):
        qkv_ref, lse_ref = loads.pop(), loads.pop()
        dctx = dctx_all[:, index * LANE : (index + 1) * LANE]
        query, key, value = (qkv_ref[:, i * LANE : (i + 1) * LANE] for i in range(3))
        query = query * jnp.asarray(SCALE, BF)
        key_t = key.T
        parts = []
        for head in range(2):
            mine = lane >= HDIM if head else lane < HDIM
            scores = dot_nt(jnp.where(mine, key, jnp.zeros_like(key)), query) + bias
            prob = jnp.exp(scores - lse_ref[head : head + 1, :])
            d_prob = dot_nt(jnp.where(mine, value, jnp.zeros_like(value)), dctx)
            inner = jnp.sum(prob * d_prob, axis=0, keepdims=True)
            d_scores = (prob * (d_prob - inner)).astype(BF)
            parts.append(
                (dot(key_t, d_scores), dot(d_scores, query), dot(prob.astype(BF), dctx))
            )
        d_query = (jnp.where(line < HDIM, parts[0][0], parts[1][0]) * SCALE).astype(BF).T
        d_key = jnp.where(lane < HDIM, parts[0][1], parts[1][1]).astype(BF)
        d_value = jnp.where(lane < HDIM, parts[0][2], parts[1][2]).astype(BF)
        grads.append(jnp.concatenate([d_query, d_key, d_value], axis=1))
    both = jnp.concatenate(grads, axis=1)
    datt_t, tok_t = loads.pop()[...], loads.pop()[...]
    ctx = jnp.concatenate([loads.pop()[...] for _ in range(2)], axis=1)
    qkv_grad = dot(tok_t, both)
    out_grad = dot(datt_t, ctx)
    half = tok_t.shape[0] // 2
    for unit in range(2):
        full = jnp.concatenate(
            [
                qkv_grad[:, unit * 3 * LANE : (unit + 1) * 3 * LANE],
                out_grad[:, unit * LANE : (unit + 1) * LANE],
            ],
            axis=1,
        )
        if has_recv:
            full = full + loads.pop()[...].astype(F32)
        full = full.astype(BF)
        if near:
            stores.part(0, full[:, : 2 * LANE], unit)
            stores.send(0, unit)
            stores.part(1, full[:half, 2 * LANE :], unit)
            stores.send(1, unit)
            stores.part(2, full[half:, 2 * LANE :], unit)
            stores.send(2, unit)
        else:
            stores.part(0, full, unit)
            stores.send(0, unit)
    wqkv = jnp.concatenate([qkv_part(kind, loads.get(slot)) for slot, _ in weights], axis=1)
    stores.put(3 if near else 1, loads.pop()[...] + dot_nt(both, wqkv))


def swap(value, axis, bit):
    count = lax.axis_size(axis)
    return lax.ppermute(value, axis, [(i, i ^ bit) for i in range(count)])


def add(*values):
    total = values[0].astype(F32)
    for value in values[1:]:
        total = total + value.astype(F32)
    return total.astype(BF)


def crossed(value):
    return jnp.concatenate([value[1:], value[:1]], axis=0)


def body(
    tokens,
    segment_ids,
    qkv_weight,
    out_weight,
    up_weight,
    down_weight,
    gain_attn,
    shift_attn,
    gain_ffn,
    shift_ffn,
    cotangent,
):
    count, width = tokens.shape
    seq, tp = lax.axis_size("seq"), lax.axis_size("tp")
    me_seq, me_tp = lax.axis_index("seq"), lax.axis_index("tp")
    blocks = width // LANE
    fast = seq == blocks and seq == 8 and tp == 4 and qkv_weight.shape[2] == 2 * LANE
    hidden = up_weight.shape[1] * tp // blocks
    seg = lax.dynamic_slice_in_dim(segment_ids, me_tp, 1, axis=0)
    seg_col = seg.reshape(count, 1)
    gains = [g.reshape(1, width) for g in (gain_attn, shift_attn, gain_ffn, shift_ffn)]
    absolute = jnp.arange(blocks, dtype=jnp.int32)
    side = lax.rem(me_seq, 2)
    pairs = blocks // 2
    half = width // 2
    wide = (count, width)
    if fast:
        rel = absolute ^ me_seq
        pos = (rel & 1) * 4 + ((rel >> 1) & 1) * 2 + (rel >> 2)
        scal = jnp.concatenate([pos, side.reshape(1)]).astype(jnp.int32)
        whole = [qkv_weight, out_weight, up_weight, down_weight]
        near = [swap(w, "tp", 1) for w in whole]
        units = {(0, h): ("whole", *whole, ("side", h)) for h in range(2)}
        units.update({(1, h): ("whole", *near, ("side", h)) for h in range(2)})
        cut = call(
            cut_kernel, attn_needs(units[0, 0]), [((width, 4 * LANE), BF)], scal, [], "cut", 1
        )[0]
        mine = [
            cut,
            lax.dynamic_slice_in_dim(up_weight, side * hidden, hidden, axis=1),
            lax.dynamic_slice_in_dim(down_weight, side * hidden, hidden, axis=0),
        ]
        far_a = [swap(w, "tp", 2) for w in mine]
        far_b = [swap(w, "seq", 1) for w in far_a]
        units[2, 0], units[2, 1] = ("half", *far_a), ("half", *far_b)
        units[3, 0] = ("half", *[swap(w, "tp", 1) for w in far_a])
        units[3, 1] = ("half", *[swap(w, "tp", 1) for w in far_b])
        groups = [[(0, 0), (0, 1)], [(1, 0), (1, 1)], [(2, 0), (3, 0)], [(2, 1), (3, 1)]]
    else:
        scal = jnp.concatenate([absolute, jnp.zeros((max(1, SIDE + 1 - blocks),), jnp.int32)])
        whole = [
            lax.all_gather(qkv_weight, "tp", axis=2, tiled=True),
            lax.all_gather(out_weight, "tp", axis=0, tiled=True),
            lax.all_gather(up_weight, "tp", axis=1, tiled=True),
            lax.all_gather(down_weight, "tp", axis=0, tiled=True),
        ]
        units = {(k // 2, k % 2): ("whole", *whole, ("block", k)) for k in range(blocks)}
        groups = [[(j, 0), (j, 1)] for j in range(pairs)]
    work = 2 * count * width

    tok_t = call(turn_kernel, [need(tokens)], [((width, count), BF)], scal, [], "turn", 1)[0]
    kept = {}
    total = None
    for number, group in enumerate(groups):
        first, last = number == 0, number == len(groups) - 1
        needs = [need(tokens)]
        for unit in group:
            needs += attn_needs(units[unit])
        if not first:
            needs.append(need(total))
        outs = []
        for unit in group:
            outs += [((count, 3 * LANE), BF), ((count, LANE), BF), ((8, count), F32)]
        if last:
            outs += [(wide, F32), ((count, LANE), F32), (wide, BF), ((width, count), BF)]
        else:
            outs.append((wide, F32))
        small = [seg_col, seg] + (gains[:2] if last else [])
        kinds = [units[unit][0] for unit in group]
        res = call(
            functools.partial(attn_fwd_kernel, kinds, first, last),
            needs, outs, scal, small, f"attn_fwd{number}", 4 * work * LANE * 2,
        )
        for index, unit in enumerate(group):
            kept[unit] = tuple(res[index * 3 : index * 3 + 3])
        if last:
            hat, inv, low, low_t = res[-4:]
        else:
            total = res[-1]

    acts = {}
    for number, group in enumerate(groups):
        first, last = number == 0, number == len(groups) - 1
        needs = [need(low)]
        for unit in group:
            needs += [up_need(units[unit], hidden), down_need(units[unit], hidden)]
        if not first:
            needs.append(need(total))
        if last:
            needs += [need(hat), need(cotangent)]
        outs = []
        for unit in group:
            outs += [((count, hidden), BF), ((count, hidden), BF)]
        if last:
            outs += [
                (wide, BF), (wide, F32), (wide, BF), ((width, count), BF),
                ((1, width), F32), ((1, width), F32),
            ]
        else:
            outs.append((wide, F32))
        res = call(
            functools.partial(ffn_fwd_kernel, len(group), first, last),
            needs, outs, scal, gains if last else [], f"ffn_fwd{number}", 4 * work * hidden,
        )
        for index, unit in enumerate(group):
            acts[unit] = tuple(res[index * 2 : index * 2 + 2])
        if last:
            mixed, d_pre, d_ffn, d_ffn_t, g_gain2, g_shift2 = res[-6:]
        else:
            total = res[-1]

    order = [3, 1, 2, 0] if fast else list(range(pairs))
    ffn_g, attn_g = {}, {}
    total = d_pre
    for number, j in enumerate(order):
        last = number == len(order) - 1
        here = not fast or j % 2 == 0
        recv = swap(ffn_g[j + 1][0], "tp", 1) if fast and here else None
        needs = [need(d_ffn)]
        for h in range(2):
            unit = units[j, h]
            needs += [down_need(unit, hidden), need(acts[j, h][1])]
            if h == 0:
                needs.append(need(low_t))
                needs.append(need(d_ffn_t))
            needs.append(need(acts[j, h][0]))
            if recv is not None:
                needs.append(
                    Need(recv.shape[1:], BF, (recv, lambda ref, scal, h=h: ref.at[h], everything))
                )
            needs.append(up_need(unit, hidden))
        needs.append(need(total))
        if here:
            outs = [((2, width, hidden), BF), ((2, half, hidden), BF), ((2, half, hidden), BF)]
        else:
            outs = [((2, 2, width, hidden), BF)]
        used = 6 if here else 2
        if last:
            needs += [need(hat), need(inv)]
            outs = outs + [
                (wide, F32), (wide, BF), ((width, count), BF), ((1, width), F32), ((1, width), F32),
            ]
        else:
            outs = outs + [(wide, F32)]
        res = call(
            functools.partial(ffn_bwd_kernel, here, recv is not None, last),
            needs, outs, scal, [gains[0]] if last else [], f"ffn_bwd{j}", 8 * work * hidden,
            used + (5 if last else 1),
        )
        grads = 3 if here else 1
        ffn_g[j] = res[:grads]
        if last:
            d_pre_one, d_att, d_att_t, g_gain1, g_shift1 = res[grads:]
        else:
            total = res[grads]

    norm_grads = jnp.concatenate([g_gain1, g_shift1, g_gain2, g_shift2], axis=0)
    if fast:
        for axis, bit in (("tp", 1), ("tp", 2), ("seq", 1), ("seq", 2), ("seq", 4)):
            norm_grads = norm_grads + swap(norm_grads, axis, bit)
        share = width // (seq * tp)
        norm_grads = lax.dynamic_slice_in_dim(
            norm_grads, (me_seq * tp + me_tp) * share, share, axis=1
        )
    else:
        norm_grads = lax.psum_scatter(norm_grads, ("seq", "tp"), scatter_dimension=1, tiled=True)

    total = d_pre_one
    for j in order:
        here = not fast or j % 2 == 0
        recv = swap(attn_g[j + 1][0], "tp", 1) if fast and here else None
        needs = [need(d_att)]
        for h in range(2):
            needs += attn_needs(units[j, h])
        for h in range(2):
            needs += [need(kept[j, h][0]), need(kept[j, h][2])]
        needs += [need(d_att_t), need(tok_t)]
        needs += [need(kept[j, h][1]) for h in range(2)]
        if recv is not None:
            needs += [
                Need(recv.shape[1:], BF, (recv, lambda ref, scal, h=h: ref.at[h], everything))
                for h in range(2)
            ]
        needs.append(need(total))
        if here:
            outs = [
                ((2, width, 2 * LANE), BF), ((2, half, 2 * LANE), BF), ((2, half, 2 * LANE), BF),
            ]
        else:
            outs = [((2, width, 4 * LANE), BF)]
        used = 6 if here else 2
        res = call(
            functools.partial(attn_bwd_kernel, units[j, 0][0], here, recv is not None),
            needs, outs + [(wide, F32)], scal, [seg_col, seg], f"attn_bwd{j}",
            12 * work * LANE * 2, used + 1,
        )
        attn_g[j], total = res[:-1], res[-1]
    token_grad = total

    if fast:
        quarter, eighth = half // 2, half // 4

        def finish(lo):
            lo = add(lo[:, :quarter], swap(lo[:, quarter:], "seq", 2))
            return lo[:, :eighth].astype(F32) + swap(lo[:, eighth:], "seq", 4).astype(F32)

        def reduced(far, near):
            got = swap(far[0], "tp", 2)
            far_hi = swap(far[2], "seq", 1)
            near_hi = swap(near[2], "seq", 1)
            far_lo = swap(add(far[1], crossed(far_hi)), "tp", 2)
            one_hi = swap(add(near[0][:, half:], got[:, half:]), "seq", 1)
            one = finish(add(near[0][:, :half], got[:, :half], crossed(one_hi)))
            two = finish(add(near[1], crossed(near_hi), far_lo))
            return one, two

        def ordered(value):
            return jnp.where(
                side == 0,
                jnp.concatenate([value[0], value[1]], 1),
                jnp.concatenate([value[1], value[0]], 1),
            )

        down, up = reduced(ffn_g[2], ffn_g[0])
        qk, vo = reduced(attn_g[2], attn_g[0])
        down_grad = ordered(down).T
        up_grad = ordered(up)
        qkv_grad = jnp.stack(
            [ordered(qk[:, :, :LANE]), ordered(qk[:, :, LANE:]), ordered(vo[:, :, :LANE])]
        )
        out_grad = ordered(vo[:, :, LANE:]).T
    else:

        def scattered(value, tp_dim, seq_dim):
            value = lax.psum_scatter(value, "tp", scatter_dimension=tp_dim, tiled=True)
            value = lax.psum_scatter(value, "seq", scatter_dimension=seq_dim, tiled=True)
            return value.astype(F32)

        def joined(parts):
            return jnp.concatenate(parts, axis=1)

        both = [(j, h) for j in range(pairs) for h in range(2)]
        down = joined([ffn_g[j][0][h] for j, h in both])
        up = joined([jnp.concatenate([ffn_g[j][i][h] for i in (1, 2)], 0) for j, h in both])
        qk = [attn_g[j][0][h] for j, h in both]
        vo = [jnp.concatenate([attn_g[j][i][h] for i in (1, 2)], 0) for j, h in both]
        down_grad = scattered(down, 1, 0).T
        up_grad = scattered(up, 1, 0)
        qkv_grad = jnp.stack(
            [
                joined([g[:, :LANE] for g in qk]),
                joined([g[:, LANE:] for g in qk]),
                joined([g[:, :LANE] for g in vo]),
            ]
        )
        qkv_grad = scattered(qkv_grad, 2, 1)
        out_grad = scattered(joined([g[:, LANE:] for g in vo]), 1, 0).T
    return (mixed, token_grad, qkv_grad, out_grad, up_grad, down_grad, norm_grads)


def solution(mesh):
    return jax.shard_map(
        body,
        mesh=mesh,
        in_specs=(
            P(("seq", "tp"), None),
            P("seq", None),
            P(None, None, "tp"),
            P("tp", None),
            P(None, "tp"),
            P("tp", None),
            P(),
            P(),
            P(),
            P(),
            P(("seq", "tp"), None),
        ),
        out_specs=(
            P(("seq", "tp"), None),
            P(("seq", "tp"), None),
            P(None, "seq", "tp"),
            P("tp", "seq"),
            P("seq", "tp"),
            P("tp", "seq"),
            P(None, ("seq", "tp")),
        ),
        check_vma=False,
    )
```

time: 604 us -> 472 us (0.78)
  waiting for transfers between devices: 312 us -> 232 us
  local copies, waits for them, and re-layouts: 48.9 us -> 26.1 us
  between operations: 15.4 us -> 2.34 us
  starting transfers between devices: 51.9 us -> 41.3 us
  other arithmetic: 16.1 us -> 9.83 us
    unnamed x2 -> x0, waiting for transfers between devices: 131 us -> none
    ppermute x84 -> x43, waiting for transfers between devices: 181 us -> 232 us  [swap(): return lax.ppermute(value, axis, [(i, i ^ bit) for i in range(count)])]
    unnamed x216 -> x166, local copies, waits for them, and re-layouts: 42.3 us -> 21.5 us
    ppermute x84 -> x43, starting transfers between devices: 51.8 us -> 41.3 us  [swap(): return lax.ppermute(value, axis, [(i, i ^ bit) for i in range(count)])]
    convert_element_type x22 -> x12, other arithmetic: 12.9 us -> 6.31 us  [add(): return total.astype(BF)]
    pallas_call x17 -> x18, Pallas kernels: 150 us -> 152 us  [call(): pl.pallas_call(run, out_shape=[jax.ShapeDtypeStruct(shape, dtype) for sha...]
  transfers between devices with their start and end apart: 85 -> 43, of which waited for: 39 -> 19; matrix products, arithmetic and copies ran while one was open for 4% -> 3% of each run, Pallas kernels for 18% -> 26%
where the time goes in v2:
time: 472 us; the launch traced here: 464 us
  waiting for transfers between devices  232 us (49%)
  Pallas kernels  152 us (32%)
  starting transfers between devices  41.3 us (9%)
  local copies, waits for them, and re-layouts  26.1 us (6%)
  other arithmetic  9.83 us (2%)
    ppermute x43, waiting for transfers between devices, swap(): return lax.ppermute(value, axis, [(i, i ^ bit) for i in range(count)])  232 us
    pallas_call x18, Pallas kernels, call(): pl.pallas_call(run, out_shape=[jax.ShapeDtypeStruct(shape, dtype) for sha...  152 us
    ppermute x43, starting transfers between devices, swap(): return lax.ppermute(value, axis, [(i, i ^ bit) for i in range(count)])  41.3 us
    unnamed x166, local copies, waits for them, and re-layouts  21.5 us
  transfers between devices with their start and end apart: 43, of which 19 were waited for; matrix products, arithmetic and copies ran while one was open for 3% of the time, Pallas kernels for 26%

profile of v2, /device:TPU:0, one launch (start us, length us, event | category | flops | bytes accessed | tf_op | source)
XLA Modules:
  0.0 463.9 jit_solution(5791249986679890587)
XLA Ops:
  3.2 1.9 cut.1
  5.1 3.0 collective-permute-start
  11.5 2.0 collective-permute-start.8
  13.5 18.9 %collective-permute-done.refs_4_ = bf16[1024,512]{1,0:T(8,128)(2,1)} collective-permute-done((bf16[1024,512]{1,0:T(8,128)(2,1)}, bf16[1024,512]{1,0:T(8,128)(2,1)}, u32[]{:S(2)}, u32[]{:S(2)}) %collective-permute-start) | collective-permute-done | bytes 1048608 | tf_op jit(solution)/shard_map/ppermute | solution.py:439
  32.4 2.0 collective-permute-start.1
  35.3 19.6 %collective-permute-done.6.refs_2_.refs_8_ = bf16[1024,512]{1,0:T(8,128)(2,1)} collective-permute-done((bf16[1024,512]{1,0:T(8,128)(2,1)S(1)}, bf16[1024,512]{1,0:T(8,128)(2,1)}, u32[]{:S(2)}, u32[]{:S(2)}) %collective-permute-start.6) | collective-permute-done | bytes 1048608 | tf_op jit(solution)/shard_map/ppermute | solution.py:439
  54.9 21.6 %collective-permute-done.8.refs_3_.refs_2_ = bf16[512,1024]{1,0:T(8,128)(2,1)} collective-permute-done((bf16[512,1024]{1,0:T(8,128)(2,1)S(1)}, bf16[512,1024]{1,0:T(8,128)(2,1)}, u32[]{:S(2)}, u32[]{:S(2)}) %collective-permute-start.8) | collective-permute-done | bytes 1048608 | tf_op jit(solution)/shard_map/ppermute | solution.py:439
  77.7 1.7 collective-permute-start.7
  80.7 23.3 %collective-permute-done.7.refs_6_.refs_12_ = bf16[1024,512]{1,0:T(8,128)(2,1)} collective-permute-done((bf16[1024,512]{1,0:T(8,128)(2,1)}, bf16[1024,512]{1,0:T(8,128)(2,1)}, u32[]{:S(2)}, u32[]{:S(2)}) %collective-permute-start.7) | collective-permute-done | bytes 1048608 | tf_op jit(solution)/shard_map/ppermute | solution.py:439
  104.0 22.1 %collective-permute-done.9.refs_7_.refs_9_ = bf16[512,1024]{1,0:T(8,128)(2,1)} collective-permute-done((bf16[512,1024]{1,0:T(8,128)(2,1)}, bf16[512,1024]{1,0:T(8,128)(2,1)}, u32[]{:S(2)}, u32[]{:S(2)}) %collective-permute-start.9) | collective-permute-done | bytes 1048608 | tf_op jit(solution)/shard_map/ppermute | solution.py:439
  126.9 8.0 %attn_fwd0.1 = (bf16[512,384]{1,0:T(8,128)(2,1)S(1)}, bf16[512,128]{1,0:T(8,128)(2,1)S(1)}, f32[8,512]{1,0:T(8,128)S(1)}, bf16[512,384]{1,0:T(8,128)(2,1)S(1)}, ...) custom-call(s32[9]{0:T(128)S(1)} %pad_add_fusion.refs_0_, s32[512,1]{1,0:T(8,128)S(1)} %copy.23.refs_1_, ...), custom_call_target="tpu_custom_call" | custom-call | flops 1073741824 | bytes 3145728 | tf_op jit(solution)/shard_map/attn_fwd0/pallas_call | solution.py:129
  138.9 8.1 %attn_fwd1.1 = (bf16[512,384]{1,0:T(8,128)(2,1)S(1)}, bf16[512,128]{1,0:T(8,128)(2,1)S(1)}, f32[8,512]{1,0:T(8,128)S(1)}, bf16[512,384]{1,0:T(8,128)(2,1)S(1)}, ...) custom-call(s32[9]{0:T(128)S(1)} %pad_add_fusion.refs_0_, s32[512,1]{1,0:T(8,128)S(1)} %copy.23.refs_1_, ...), custom_call_target="tpu_custom_call" | custom-call | flops 1073741824 | bytes 5242880 | tf_op jit(solution)/shard_map/attn_fwd1/pallas_call | solution.py:129
  148.5 9.2 %attn_fwd2.1 = (bf16[512,384]{1,0:T(8,128)(2,1)S(1)}, bf16[512,128]{1,0:T(8,128)(2,1)S(1)}, f32[8,512]{1,0:T(8,128)S(1)}, bf16[512,384]{1,0:T(8,128)(2,1)S(1)}, ...) custom-call(s32[9]{0:T(128)S(1)} %pad_add_fusion.refs_0_, s32[512,1]{1,0:T(8,128)S(1)} %copy.23.refs_1_, ...), custom_call_target="tpu_custom_call" | custom-call | flops 1073741824 | bytes 5242880 | tf_op jit(solution)/shard_map/attn_fwd2/pallas_call | solution.py:129
  158.9 9.6 %attn_fwd3.1 = (bf16[512,384]{1,0:T(8,128)(2,1)S(1)}, bf16[512,128]{1,0:T(8,128)(2,1)S(1)}, f32[8,512]{1,0:T(8,128)S(1)}, bf16[512,384]{1,0:T(8,128)(2,1)S(1)}, ...) custom-call(s32[9]{0:T(128)S(1)} %pad_add_fusion.refs_0_, ...), custom_call_target="tpu_custom_call" | custom-call | flops 1073741824 | bytes 5242880 | tf_op jit(solution)/shard_map/attn_fwd3/pallas_call | solution.py:129
  169.9 5.8 %ffn_fwd0.1 = (bf16[512,512]{1,0:T(8,128)(2,1)S(1)}, bf16[512,512]{1,0:T(8,128)(2,1)S(1)}, bf16[512,512]{1,0:T(8,128)(2,1)S(1)}, bf16[512,512]{1,0:T(8,128)(2,1)S(1)}, f32[512,1024]{1,0:T(8,128)S(1)}) custom-call(s32[9]{0:T(128)S(1)} %pad_add_fusion.refs_0_, bf16[512,1024]{1,0:T(8,128)(2,1)S(1)} %get-tuple-element.94.refs_1_.refs_5_, ...), custom_call_target="tpu_custom_call" | custom-call | flops 2147483648 | bytes 5242880 | tf_op jit(solution)/shard_map/ffn_fwd0/pallas_call | solution.py:129
  177.0 6.2 %ffn_fwd1.1 = (bf16[512,512]{1,0:T(8,128)(2,1)S(1)}, bf16[512,512]{1,0:T(8,128)(2,1)S(1)}, bf16[512,512]{1,0:T(8,128)(2,1)S(1)}, bf16[512,512]{1,0:T(8,128)(2,1)S(1)}, f32[512,1024]{1,0:T(8,128)S(1)}) custom-call(s32[9]{0:T(128)S(1)} %pad_add_fusion.refs_0_, bf16[512,1024]{1,0:T(8,128)(2,1)S(1)} %get-tuple-element.94.refs_1_.refs_5_, ...), custom_call_target="tpu_custom_call" | custom-call | flops 2147483648 | bytes 7340032 | tf_op jit(solution)/shard_map/ffn_fwd1/pallas_call | solution.py:129
  184.5 7.2 %ffn_fwd2.1 = (bf16[512,512]{1,0:T(8,128)(2,1)S(1)}, bf16[512,512]{1,0:T(8,128)(2,1)S(1)}, bf16[512,512]{1,0:T(8,128)(2,1)S(1)}, bf16[512,512]{1,0:T(8,128)(2,1)S(1)}, f32[512,1024]{1,0:T(8,128)}) custom-call(s32[9]{0:T(128)S(1)} %pad_add_fusion.refs_0_, bf16[512,1024]{1,0:T(8,128)(2,1)S(1)} %get-tuple-element.94.refs_1_.refs_5_, ...), custom_call_target="tpu_custom_call" | custom-call | flops 2147483648 | bytes 7340032 | tf_op jit(solution)/shard_map/ffn_fwd2/pallas_call | solution.py:129
  193.4 9.4 %ffn_fwd3.1 = (bf16[512,512]{1,0:T(8,128)(2,1)S(1)}, bf16[512,512]{1,0:T(8,128)(2,1)S(1)}, bf16[512,512]{1,0:T(8,128)(2,1)S(1)}, bf16[512,512]{1,0:T(8,128)(2,1)...) custom-call(s32[9]{0:T(128)S(1)} %pad_add_fusion.refs_0_, ...), custom_call_target="tpu_custom_call" | custom-call | flops 2147483648 | bytes 10485760 | tf_op jit(solution)/shard_map/ffn_fwd3/pallas_call | solution.py:129
  203.8 9.6 %ffn_bwd3.1 = (bf16[2,2,1024,512]{3,2,1,0:T(8,128)(2,1)}, f32[512,1024]{1,0:T(8,128)}) custom-call(s32[9]{0:T(128)S(1)} %pad_add_fusion.refs_0_, bf16[512,1024]{1,0:T(8,128)(2,1)S(1)} %get-tuple-element.100.refs_1_.refs_2_, bf16[512,1024]{1,0:T(8,128)(2,1)} %collective-permute-done.13.refs_5_.refs_2_, bf16[512,512]{1,0:T(8,128)(2,1)S(1)} %copy-done.67, ...), custom_call_target="tpu_custom_call" | custom-call | flops 4294967296 | bytes 11534336 | tf_op jit(solution)/shard_map/ffn_bwd3/pallas_call | solution.py:129
  213.9 9.2 %ffn_bwd1.1 = (bf16[2,2,1024,512]{3,2,1,0:T(8,128)(2,1)}, f32[512,1024]{1,0:T(8,128)}) custom-call(s32[9]{0:T(128)S(1)} %pad_add_fusion.refs_0_, bf16[512,1024]{1,0:T(8,128)(2,1)S(1)} %get-tuple-element.100.refs_1_.refs_2_, bf16[1024,1024]{1,0:T(8,128)(2,1)} %collective-permute-done.15.refs_3_.refs_2_, bf16[512,512]{1,0:T(8,128)(2,1)S(1)} %get-tuple-element.105.refs_3_, ...), custom_call_target="tpu_custom_call" | custom-call | flops 4294967296 | bytes 11534336 | tf_op jit(solution)/shard_map/ffn_bwd1/pallas_call | solution.py:129
  223.3 10.2 %ffn_bwd2.1 = (bf16[2,1024,512]{2,1,0:T(8,128)(2,1)}, bf16[2,512,512]{2,1,0:T(8,128)(2,1)S(1)}, bf16[2,512,512]{2,1,0:T(8,128)(2,1)S(1)}, f32[512,1024]{1,0:T(8,128)}) custom-call(s32[9]{0:T(128)S(1)} %pad_add_fusion.refs_0_, bf16[512,1024]{1,0:T(8,128)(2,1)S(1)} %get-tuple-element.100.refs_1_.refs_2_, ...), custom_call_target="tpu_custom_call" | custom-call | flops 4294967296 | bytes 15728640 | tf_op jit(solution)/shard_map/ffn_bwd2/pallas_call | solution.py:129
  233.5 11.8 %ffn_bwd0.1 = (bf16[2,1024,512]{2,1,0:T(8,128)(2,1)}, bf16[2,512,512]{2,1,0:T(8,128)(2,1)S(1)}, bf16[2,512,512]{2,1,0:T(8,128)(2,1)}, f32[512,1024]{1,0:T(8,128)...) custom-call(s32[9]{0:T(128)S(1)} %pad_add_fusion.refs_0_, ...), custom_call_target="tpu_custom_call" | custom-call | flops 4294967296 | bytes 18087936 | tf_op jit(solution)/shard_map/ffn_bwd0/pallas_call | solution.py:129
  245.9 1.7 collective-permute-start.30
  252.5 10.8 %attn_bwd3.1 = (bf16[2,1024,512]{2,1,0:T(8,128)(2,1)}, f32[512,1024]{1,0:T(8,128)}) custom-call(s32[9]{0:T(128)S(1)} %pad_add_fusion.refs_0_, s32[512,1]{1,0:T(8,128)S(1)} %copy.23.refs_1_, s32[1,512]{1,0:T(1,128)S(1)} %constant_dynamic-slice_fusion.2.refs_2_, bf16[512,1024]{1,0:T(8,128)(2,1)S(1)} %get-tuple-element.126.refs_3_, ...), custom_call_target="tpu_custom_call" | custom-call | flops 3221225472 | bytes 8421376 | tf_op jit(solution)/shard_map/attn_bwd3/pallas_call | solution.py:129
  263.4 8.0 %collective-permute-done.40 = f32[4,1024]{1,0:T(4,128)S(1)} collective-permute-done((f32[4,1024]{1,0:T(4,128)S(1)}, f32[4,1024]{1,0:T(4,128)S(1)}, u32[]{:S(2)}, u32[]{:S(2)}) %collective-permute-start.40) | collective-permute-done | bytes 16416 | tf_op jit(solution)/shard_map/ppermute | solution.py:439
  271.4 1.8 collective-permute-start.41
  273.2 11.0 %attn_bwd1.1 = (bf16[2,1024,512]{2,1,0:T(8,128)(2,1)}, f32[512,1024]{1,0:T(8,128)}) custom-call(s32[9]{0:T(128)S(1)} %pad_add_fusion.refs_0_, s32[512,1]{1,0:T(8,128)S(1)} %copy.23.refs_1_, s32[1,512]{1,0:T(1,128)S(1)} %constant_dynamic-slice_fusion.2.refs_2_, bf16[512,1024]{1,0:T(8,128)(2,1)S(1)} %get-tuple-element.126.refs_3_, ...), custom_call_target="tpu_custom_call" | custom-call | flops 3221225472 | bytes 8421376 | tf_op jit(solution)/shard_map/attn_bwd1/pallas_call | solution.py:129
  287.4 2.7 collective-permute-start.42
  290.5 1.8 collective-permute-done.42
  294.1 16.1 %collective-permute-done.29 = bf16[2,512,512]{2,1,0:T(8,128)(2,1)} collective-permute-done((bf16[2,512,512]{2,1,0:T(8,128)(2,1)}, bf16[2,512,512]{2,1,0:T(8,128)(2,1)}, u32[]{:S(2)}, u32[]{:S(2)}) %collective-permute-start.29) | collective-permute-done | bytes 1048608 | tf_op jit(solution)/shard_map/ppermute | solution.py:439
  311.5 44.9 %collective-permute-done.31 = bf16[2,512,512]{2,1,0:T(8,128)(2,1)} collective-permute-done((bf16[2,512,512]{2,1,0:T(8,128)(2,1)S(1)}, bf16[2,512,512]{2,1,0:T(8,128)(2,1)}, u32[]{:S(2)}, u32[]{:S(2)}) %collective-permute-start.31) | collective-permute-done | bytes 1048608 | tf_op jit(solution)/shard_map/ppermute | solution.py:439
  356.4 1.8 add_convert_fusion.2
  358.8 11.8 %attn_bwd2.1 = (bf16[2,1024,256]{2,1,0:T(8,128)(2,1)S(1)}, bf16[2,512,256]{2,1,0:T(8,128)(2,1)S(1)}, bf16[2,512,256]{2,1,0:T(8,128)(2,1)S(1)}, f32[512,1024]{1,0:T(8,128)}) custom-call(s32[9]{0:T(128)S(1)} %pad_add_fusion.refs_0_, s32[512,1]{1,0:T(8,128)S(1)} %copy.23.refs_1_, s32[1,512]{1,0:T(1,128)S(1)} %constant_dynamic-slice_fusion.2.refs_2_, ...), custom_call_target="tpu_custom_call" | custom-call | flops 3221225472 | bytes 10518528 | tf_op jit(solution)/shard_map/attn_bwd2/pallas_call | solution.py:129
  371.1 11.7 %attn_bwd0.1 = (bf16[2,1024,256]{2,1,0:T(8,128)(2,1)S(1)}, bf16[2,512,256]{2,1,0:T(8,128)(2,1)S(1)}, bf16[2,512,256]{2,1,0:T(8,128)(2,1)S(1)}, f32[512,1024]{1,0:T(8,128)}) custom-call(s32[9]{0:T(128)S(1)} %pad_add_fusion.refs_0_, s32[512,1]{1,0:T(8,128)S(1)} %copy.23.refs_1_, s32[1,512]{1,0:T(1,128)S(1)} %constant_dynamic-slice_fusion.2.refs_2_, ...), custom_call_target="tpu_custom_call" | custom-call | flops 3221225472 | bytes 10518528 | tf_op jit(solution)/shard_map/attn_bwd0/pallas_call | solution.py:129
  382.8 1.8 collective-permute-start.24
  388.4 2.7 collective-permute-start.33
  391.8 5.9 %collective-permute-done.24 = bf16[2,512,256]{2,1,0:T(8,128)(2,1)S(1)} collective-permute-done((bf16[2,512,256]{2,1,0:T(8,128)(2,1)S(1)}, bf16[2,512,256]{2,1,0:T(8,128)(2,1)S(1)}, u32[]{:S(2)}, u32[]{:S(2)}) %collective-permute-start.24) | collective-permute-done | bytes 524320 | tf_op jit(solution)/shard_map/ppermute | solution.py:439
  397.8 3.3 collective-permute-done.33
  401.2 9.4 %collective-permute-done.20 = bf16[2,1024,256]{2,1,0:T(8,128)(2,1)S(1)} collective-permute-done((bf16[2,1024,256]{2,1,0:T(8,128)(2,1)S(1)}, bf16[2,1024,256]{2,1,0:T(8,128)(2,1)S(1)}, u32[]{:S(2)}, u32[]{:S(2)}) %collective-permute-start.20) | collective-permute-done | bytes 1048608 | tf_op jit(solution)/shard_map/ppermute | solution.py:439
  411.2 8.2 %collective-permute-done.26 = bf16[2,512,256]{2,1,0:T(8,128)(2,1)S(1)} collective-permute-done((bf16[2,512,256]{2,1,0:T(8,128)(2,1)S(1)}, bf16[2,512,256]{2,1,0:T(8,128)(2,1)S(1)}, u32[]{:S(2)}, u32[]{:S(2)}) %collective-permute-start.26) | collective-permute-done | bytes 524320 | tf_op jit(solution)/shard_map/ppermute | solution.py:439
  419.6 1.6 collective-permute-start.27
  421.3 4.7 %collective-permute-done.27 = bf16[2,256,256]{2,1,0:T(8,128)(2,1)S(1)} collective-permute-done((bf16[2,256,256]{2,1,0:T(8,128)(2,1)S(1)}, bf16[2,256,256]{2,1,0:T(8,128)(2,1)S(1)}, u32[]{:S(2)}, u32[]{:S(2)}) %collective-permute-start.27) | collective-permute-done | bytes 262176 | tf_op jit(solution)/shard_map/ppermute | solution.py:439
  426.2 3.3 collective-permute-start.28
  429.4 1.6 add_convert_fusion
  433.7 1.8 collective-permute-start.22
  435.6 12.3 %collective-permute-done.36 = bf16[2,256,512]{2,1,0:T(8,128)(2,1)S(1)} collective-permute-done((bf16[2,256,512]{2,1,0:T(8,128)(2,1)S(1)}, bf16[2,256,512]{2,1,0:T(8,128)(2,1)S(1)}, u32[]{:S(2)}, u32[]{:S(2)}) %collective-permute-start.36) | collective-permute-done | bytes 524320 | tf_op jit(solution)/shard_map/ppermute | solution.py:439
  448.9 1.8 collective-permute-done.22
  451.9 8.5 %collective-permute-done.37 = bf16[2,128,512]{2,1,0:T(8,128)(2,1)S(1)} collective-permute-done((bf16[2,128,512]{2,1,0:T(8,128)(2,1)S(1)}, bf16[2,128,512]{2,1,0:T(8,128)(2,1)S(1)}, u32[]{:S(2)}, u32[]{:S(2)}) %collective-permute-start.37) | collective-permute-done | bytes 262176 | tf_op jit(solution)/shard_map/ppermute | solution.py:439
  (274 shorter events, 50.2 us)
Async XLA Ops:
  0.6 125.4 %copy-start = (s32[4,512]{1,0:T(4,128)S(1)}, s32[4,512]{1,0:T(4,128)}, u32[]{:S(2)}) copy-start(s32[4,512]{1,0:T(4,128)} %param.12) | copy-start | bytes 24580
  5.1 27.3 %collective-permute-start = (bf16[1024,512]{1,0:T(8,128)(2,1)}, bf16[1024,512]{1,0:T(8,128)(2,1)}, u32[]{:S(2)}, u32[]{:S(2)}) collective-permute-start(bf16[1024,512]{1,0:T(8,128)(2,1)} %cut.1), channel_id=1, source_target_pairs={{0,2},{1,3},{2,0},{3,1},{4,6},{5,7},{6,4},{7,5},{8,10},{9,11},{10,... | collective-permute-start | bytes 3145736 | tf_op jit(solution)/shard_map/ppermute | solution.py:439
  8.1 118.8 %copy-start.2 = (bf16[512,1024]{1,0:T(8,128)(2,1)S(1)}, bf16[512,1024]{1,0:T(8,128)(2,1)}, u32[]{:S(2)}) copy-start(bf16[512,1024]{1,0:T(8,128)(2,1)} %refs_1_.3) | copy-start | bytes 3145732
  9.5 45.4 %collective-permute-start.6 = (bf16[1024,512]{1,0:T(8,128)(2,1)S(1)}, bf16[1024,512]{1,0:T(8,128)(2,1)}, u32[]{:S(2)}, u32[]{:S(2)}) collective-permute-start(bf16[1024,512]{1,0:T(8,128)(2,1)S(1)} %constant_dynamic-slice_fusion.1), channel_id=1, source_target_pairs={{0,2},{1,3},{2,0},{3,1},{4,6},{5,7},{6,4},{7,5},{8,10},{9,11},{10,... | collective-permute-start | bytes 3145736 | tf_op jit(solution)/shard_map/ppermute | solution.py:439
  9.6 66.9 %collective-permute-start.4 = (bf16[3,1024,256]{2,1,0:T(8,128)(2,1)S(1)}, bf16[3,1024,256]{2,1,0:T(8,128)(2,1)S(1)}, u32[]{:S(2)}, u32[]{:S(2)}) collective-permute-start(bf16[3,1024,256]{2,1,0:T(8,128)(2,1)S(1)} %copy-done.4), channel_id=1, source_target_pairs={{0,1},{1,0},{2,3},{3,2},{4,5},{5,4},{6,7},{7,6},{8,9},{9,8},{10,11... | collective-permute-start | bytes 4718600 | tf_op jit(solution)/shard_map/ppermute | solution.py:439
  9.7 24.8 %collective-permute-start.5 = (bf16[256,1024]{1,0:T(8,128)(2,1)S(1)}, bf16[256,1024]{1,0:T(8,128)(2,1)S(1)}, u32[]{:S(2)}, u32[]{:S(2)}) collective-permute-start(bf16[256,1024]{1,0:T(8,128)(2,1)S(1)} %copy-done.16), channel_id=1, source_target_pairs={{0,1},{1,0},{2,3},{3,2},{4,5},{5,4},{6,7},{7,6},{8,9},{9,8},{10,11... | collective-permute-start | bytes 1572872 | tf_op jit(solution)/shard_map/ppermute | solution.py:439
  11.5 65.1 %collective-permute-start.8 = (bf16[512,1024]{1,0:T(8,128)(2,1)S(1)}, bf16[512,1024]{1,0:T(8,128)(2,1)}, u32[]{:S(2)}, u32[]{:S(2)}) collective-permute-start(bf16[512,1024]{1,0:T(8,128)(2,1)S(1)} %constant_dynamic-slice_fusion), channel_id=1, source_target_pairs={{0,2},{1,3},{2,0},{3,1},{4,6},{5,7},{6,4},{7,5},{8,10},{9,11},{10,... | collective-permute-start | bytes 3145736 | tf_op jit(solution)/shard_map/ppermute | solution.py:439
  32.4 47.0 %collective-permute-start.1 = (bf16[1024,512]{1,0:T(8,128)(2,1)}, bf16[1024,512]{1,0:T(8,128)(2,1)}, u32[]{:S(2)}, u32[]{:S(2)}) collective-permute-start(bf16[1024,512]{1,0:T(8,128)(2,1)} %collective-permute-done.refs_4_), channel_id=1, source_target_pairs={{0,4},{4,0},{8,12},{12,8},{16,20},{20,16},{24,28},{28,24},{1,5},{5... | collective-permute-start | bytes 3145736 | tf_op jit(solution)/shard_map/ppermute | solution.py:439
  35.3 90.8 %collective-permute-start.14 = (bf16[1024,1024]{1,0:T(8,128)(2,1)}, bf16[1024,1024]{1,0:T(8,128)(2,1)}, u32[]{:S(2)}, u32[]{:S(2)}) collective-permute-start(bf16[1024,1024]{1,0:T(8,128)(2,1)} %refs_9_.1), channel_id=1, source_target_pairs={{0,1},{1,0},{2,3},{3,2},{4,5},{5,4},{6,7},{7,6},{8,9},{9,8},{10,11... | collective-permute-start | bytes 6291464 | tf_op jit(solution)/shard_map/ppermute | solution.py:439
  54.9 24.8 %collective-permute-start.3 = (bf16[1024,512]{1,0:T(8,128)(2,1)}, bf16[1024,512]{1,0:T(8,128)(2,1)S(1)}, u32[]{:S(2)}, u32[]{:S(2)}) collective-permute-start(bf16[1024,512]{1,0:T(8,128)(2,1)} %collective-permute-done.refs_4_), channel_id=1, source_target_pairs={{0,1},{1,0},{2,3},{3,2},{4,5},{5,4},{6,7},{7,6},{8,9},{9,8},{10,11... | collective-permute-start | bytes 3145736 | tf_op jit(solution)/shard_map/ppermute | solution.py:439
  76.5 100.5 %collective-permute-start.15 = (bf16[1024,1024]{1,0:T(8,128)(2,1)}, bf16[1024,1024]{1,0:T(8,128)(2,1)}, u32[]{:S(2)}, u32[]{:S(2)}) collective-permute-start(bf16[1024,1024]{1,0:T(8,128)(2,1)} %refs_3_.9), channel_id=1, source_target_pairs={{0,1},{1,0},{2,3},{3,2},{4,5},{5,4},{6,7},{7,6},{8,9},{9,8},{10,11... | collective-permute-start | bytes 6291464 | tf_op jit(solution)/shard_map/ppermute | solution.py:439
  77.7 26.3 %collective-permute-start.7 = (bf16[1024,512]{1,0:T(8,128)(2,1)}, bf16[1024,512]{1,0:T(8,128)(2,1)}, u32[]{:S(2)}, u32[]{:S(2)}) collective-permute-start(bf16[1024,512]{1,0:T(8,128)(2,1)} %collective-permute-done.6.refs_2_.refs_8_), channel_id=1, source_target_pairs={{0,4},{4,0},{8,12},{12,8},{16,20},{20,16},{24,28},{28,24},{1,5},{5... | collective-permute-start | bytes 3145736 | tf_op jit(solution)/shard_map/ppermute | solution.py:439
  79.4 46.6 %collective-permute-start.9 = (bf16[512,1024]{1,0:T(8,128)(2,1)}, bf16[512,1024]{1,0:T(8,128)(2,1)}, u32[]{:S(2)}, u32[]{:S(2)}) collective-permute-start(bf16[512,1024]{1,0:T(8,128)(2,1)} %collective-permute-done.8.refs_3_.refs_2_), channel_id=1, source_target_pairs={{0,4},{4,0},{8,12},{12,8},{16,20},{20,16},{24,28},{28,24},{1,5},{5... | collective-permute-start | bytes 3145736 | tf_op jit(solution)/shard_map/ppermute | solution.py:439
  80.7 46.0 %collective-permute-start.2 = (bf16[1024,512]{1,0:T(8,128)(2,1)}, bf16[1024,512]{1,0:T(8,128)(2,1)}, u32[]{:S(2)}, u32[]{:S(2)}) collective-permute-start(bf16[1024,512]{1,0:T(8,128)(2,1)} %collective-permute-done.1.refs_6_.refs_5_), channel_id=1, source_target_pairs={{0,1},{1,0},{2,3},{3,2},{4,5},{5,4},{6,7},{7,6},{8,9},{9,8},{10,11... | collective-permute-start | bytes 3145736 | tf_op jit(solution)/shard_map/ppermute | solution.py:439
  104.0 80.6 %collective-permute-start.12 = (bf16[1024,512]{1,0:T(8,128)(2,1)}, bf16[1024,512]{1,0:T(8,128)(2,1)}, u32[]{:S(2)}, u32[]{:S(2)}) collective-permute-start(bf16[1024,512]{1,0:T(8,128)(2,1)} %collective-permute-done.6.refs_2_.refs_8_), channel_id=1, source_target_pairs={{0,1},{1,0},{2,3},{3,2},{4,5},{5,4},{6,7},{7,6},{8,9},{9,8},{10,11... | collective-permute-start | bytes 3145736 | tf_op jit(solution)/shard_map/ppermute | solution.py:439
  126.0 58.5 %collective-permute-start.13 = (bf16[512,1024]{1,0:T(8,128)(2,1)}, bf16[512,1024]{1,0:T(8,128)(2,1)}, u32[]{:S(2)}, u32[]{:S(2)}) collective-permute-start(bf16[512,1024]{1,0:T(8,128)(2,1)} %collective-permute-done.8.refs_3_.refs_2_), channel_id=1, source_target_pairs={{0,1},{1,0},{2,3},{3,2},{4,5},{5,4},{6,7},{7,6},{8,9},{9,8},{10,11... | collective-permute-start | bytes 3145736 | tf_op jit(solution)/shard_map/ppermute | solution.py:439
  126.1 67.3 %collective-permute-start.10 = (bf16[1024,512]{1,0:T(8,128)(2,1)}, bf16[1024,512]{1,0:T(8,128)(2,1)}, u32[]{:S(2)}, u32[]{:S(2)}) collective-permute-start(bf16[1024,512]{1,0:T(8,128)(2,1)} %collective-permute-done.7.refs_6_.refs_12_), channel_id=1, source_target_pairs={{0,1},{1,0},{2,3},{3,2},{4,5},{5,4},{6,7},{7,6},{8,9},{9,8},{10,11... | collective-permute-start | bytes 3145736 | tf_op jit(solution)/shard_map/ppermute | solution.py:439
  126.6 66.7 %collective-permute-start.11 = (bf16[512,1024]{1,0:T(8,128)(2,1)}, bf16[512,1024]{1,0:T(8,128)(2,1)}, u32[]{:S(2)}, u32[]{:S(2)}) collective-permute-start(bf16[512,1024]{1,0:T(8,128)(2,1)} %collective-permute-done.9.refs_7_.refs_9_), channel_id=1, source_target_pairs={{0,1},{1,0},{2,3},{3,2},{4,5},{5,4},{6,7},{7,6},{8,9},{9,8},{10,11... | collective-permute-start | bytes 3145736 | tf_op jit(solution)/shard_map/ppermute | solution.py:439
  169.9 44.0 %copy-start.7 = (bf16[1024,512]{1,0:T(8,128)(2,1)}, bf16[1024,512]{1,0:T(8,128)(2,1)S(1)}, u32[]{:S(2)}) copy-start(bf16[1024,512]{1,0:T(8,128)(2,1)S(1)} %get-tuple-element.102.refs_4_.refs_5_) | copy-start | bytes 3145732
  213.4 9.9 %collective-permute-start.17 = (bf16[2,2,1024,512]{3,2,1,0:T(8,128)(2,1)}, bf16[2,2,1024,512]{3,2,1,0:T(8,128)(2,1)}, u32[]{:S(2)}, u32[]{:S(2)}) collective-permute-start(bf16[2,2,1024,512]{3,2,1,0:T(8,128)(2,1)} %get-tuple-element.120), channel_id=1, source_target_pairs={{0,1},{1,0},{2,3},{3,2},{4,5},{5,4},{6,7},{7,6},{8,9},{9,8},{10,11... | collective-permute-start | bytes 12582920 | tf_op jit(solution)/shard_map/ppermute | solution.py:439
  223.1 10.4 %collective-permute-start.16 = (bf16[2,2,1024,512]{3,2,1,0:T(8,128)(2,1)}, bf16[2,2,1024,512]{3,2,1,0:T(8,128)(2,1)}, u32[]{:S(2)}, u32[]{:S(2)}) collective-permute-start(bf16[2,2,1024,512]{3,2,1,0:T(8,128)(2,1)} %get-tuple-element.115), channel_id=1, source_target_pairs={{0,1},{1,0},{2,3},{3,2},{4,5},{5,4},{6,7},{7,6},{8,9},{9,8},{10,11... | collective-permute-start | bytes 12582920 | tf_op jit(solution)/shard_map/ppermute | solution.py:439
  245.3 27.9 %copy-start.24 = (bf16[512,1024]{1,0:T(8,128)(2,1)}, bf16[512,1024]{1,0:T(8,128)(2,1)S(1)}, u32[]{:S(2)}) copy-start(bf16[512,1024]{1,0:T(8,128)(2,1)S(1)} %get-tuple-element.126.refs_3_) | copy-start | bytes 3145732
  245.4 2.2 collective-permute-start.38
  245.9 41.5 %collective-permute-start.30 = (bf16[2,512,512]{2,1,0:T(8,128)(2,1)S(1)}, bf16[2,512,512]{2,1,0:T(8,128)(2,1)S(1)}, u32[]{:S(2)}, u32[]{:S(2)}) collective-permute-start(bf16[2,512,512]{2,1,0:T(8,128)(2,1)S(1)} %get-tuple-element.168), channel_id=1, source_target_pairs={{0,4},{4,0},{8,12},{12,8},{16,20},{20,16},{24,28},{28,24},{1,5},{5... | collective-permute-start | bytes 3145736 | tf_op jit(solution)/shard_map/ppermute | solution.py:439
  247.6 3.8 collective-permute-start.39
  251.4 19.9 %collective-permute-start.40 = (f32[4,1024]{1,0:T(4,128)S(1)}, f32[4,1024]{1,0:T(4,128)S(1)}, u32[]{:S(2)}, u32[]{:S(2)}) collective-permute-start(f32[4,1024]{1,0:T(4,128)S(1)} %fusion.10), channel_id=1, source_target_pairs={{0,4},{4,0},{8,12},{12,8},{16,20},{20,16},{24,28},{28,24},{1,5},{5... | collective-permute-start | bytes 49160 | tf_op jit(solution)/shard_map/ppermute | solution.py:439
  252.4 20.8 %copy-start.12 = (bf16[1024,512]{1,0:T(8,128)(2,1)S(1)}, bf16[1024,512]{1,0:T(8,128)(2,1)}, u32[]{:S(2)}) copy-start(bf16[1024,512]{1,0:T(8,128)(2,1)} %copy-done.11) | copy-start | bytes 3145732
  263.3 95.4 %collective-permute-start.19 = (bf16[2,1024,512]{2,1,0:T(8,128)(2,1)}, bf16[2,1024,512]{2,1,0:T(8,128)(2,1)}, u32[]{:S(2)}, u32[]{:S(2)}) collective-permute-start(bf16[2,1024,512]{2,1,0:T(8,128)(2,1)} %get-tuple-element.155), channel_id=1, source_target_pairs={{0,1},{1,0},{2,3},{3,2},{4,5},{5,4},{6,7},{7,6},{8,9},{9,8},{10,11... | collective-permute-start | bytes 6291464 | tf_op jit(solution)/shard_map/ppermute | solution.py:439
  271.4 14.5 %collective-permute-start.41 = (f32[4,1024]{1,0:T(4,128)S(1)}, f32[4,1024]{1,0:T(4,128)S(1)}, u32[]{:S(2)}, u32[]{:S(2)}) collective-permute-start(f32[4,1024]{1,0:T(4,128)S(1)} %add.120), channel_id=1, source_target_pairs={{0,8},{4,12},{8,0},{12,4},{16,24},{20,28},{24,16},{28,20},{1,9},{5... | collective-permute-start | bytes 49160 | tf_op jit(solution)/shard_map/ppermute | solution.py:439
  284.2 86.7 %collective-permute-start.18 = (bf16[2,1024,512]{2,1,0:T(8,128)(2,1)}, bf16[2,1024,512]{2,1,0:T(8,128)(2,1)}, u32[]{:S(2)}, u32[]{:S(2)}) collective-permute-start(bf16[2,1024,512]{2,1,0:T(8,128)(2,1)} %get-tuple-element.148), channel_id=1, source_target_pairs={{0,1},{1,0},{2,3},{3,2},{4,5},{5,4},{6,7},{7,6},{8,9},{9,8},{10,11... | collective-permute-start | bytes 6291464 | tf_op jit(solution)/shard_map/ppermute | solution.py:439
  284.3 25.9 %collective-permute-start.29 = (bf16[2,512,512]{2,1,0:T(8,128)(2,1)}, bf16[2,512,512]{2,1,0:T(8,128)(2,1)}, u32[]{:S(2)}, u32[]{:S(2)}) collective-permute-start(bf16[2,512,512]{2,1,0:T(8,128)(2,1)} %get-tuple-element.166), channel_id=1, source_target_pairs={{0,4},{4,0},{8,12},{12,8},{16,20},{20,16},{24,28},{28,24},{1,5},{5... | collective-permute-start | bytes 3145736 | tf_op jit(solution)/shard_map/ppermute | solution.py:439
  285.9 100.2 %collective-permute-start.34 = (bf16[2,1024,512]{2,1,0:T(8,128)(2,1)}, bf16[2,1024,512]{2,1,0:T(8,128)(2,1)}, u32[]{:S(2)}, u32[]{:S(2)}) collective-permute-start(bf16[2,1024,512]{2,1,0:T(8,128)(2,1)} %get-tuple-element.170), channel_id=1, source_target_pairs={{0,2},{1,3},{2,0},{3,1},{4,6},{5,7},{6,4},{7,5},{8,10},{9,11},{10,... | collective-permute-start | bytes 6291464 | tf_op jit(solution)/shard_map/ppermute | solution.py:439
  287.4 4.9 %collective-permute-start.42 = (f32[4,1024]{1,0:T(4,128)S(1)}, f32[4,1024]{1,0:T(4,128)}, u32[]{:S(2)}, u32[]{:S(2)}) collective-permute-start(f32[4,1024]{1,0:T(4,128)S(1)} %add.121), channel_id=1, source_target_pairs={{0,16},{4,20},{8,24},{12,28},{16,0},{20,4},{24,8},{28,12},{1,17},{... | collective-permute-start | bytes 49160 | tf_op jit(solution)/shard_map/ppermute | solution.py:439
  292.3 64.1 %collective-permute-start.31 = (bf16[2,512,512]{2,1,0:T(8,128)(2,1)S(1)}, bf16[2,512,512]{2,1,0:T(8,128)(2,1)}, u32[]{:S(2)}, u32[]{:S(2)}) collective-permute-start(bf16[2,512,512]{2,1,0:T(8,128)(2,1)S(1)} %add_convert_fusion.3), channel_id=1, source_target_pairs={{0,2},{1,3},{2,0},{3,1},{4,6},{5,7},{6,4},{7,5},{8,10},{9,11},{10,... | collective-permute-start | bytes 3145736 | tf_op jit(solution)/shard_map/ppermute | solution.py:439
  358.2 30.1 %collective-permute-start.32 = (bf16[2,256,512]{2,1,0:T(8,128)(2,1)S(1)}, bf16[2,256,512]{2,1,0:T(8,128)(2,1)S(1)}, u32[]{:S(2)}, u32[]{:S(2)}) collective-permute-start(bf16[2,256,512]{2,1,0:T(8,128)(2,1)S(1)} %slice.245), channel_id=1, source_target_pairs={{0,8},{4,12},{8,0},{12,4},{16,24},{20,28},{24,16},{28,20},{1,9},{5... | collective-permute-start | bytes 1572872 | tf_op jit(solution)/shard_map/ppermute | solution.py:439
  370.6 20.5 %collective-permute-start.25 = (bf16[2,512,256]{2,1,0:T(8,128)(2,1)S(1)}, bf16[2,512,256]{2,1,0:T(8,128)(2,1)S(1)}, u32[]{:S(2)}, u32[]{:S(2)}) collective-permute-start(bf16[2,512,256]{2,1,0:T(8,128)(2,1)S(1)} %get-tuple-element.164), channel_id=1, source_target_pairs={{0,4},{4,0},{8,12},{12,8},{16,20},{20,16},{24,28},{28,24},{1,5},{5... | collective-permute-start | bytes 1572872 | tf_op jit(solution)/shard_map/ppermute | solution.py:439
  382.8 14.9 %collective-permute-start.24 = (bf16[2,512,256]{2,1,0:T(8,128)(2,1)S(1)}, bf16[2,512,256]{2,1,0:T(8,128)(2,1)S(1)}, u32[]{:S(2)}, u32[]{:S(2)}) collective-permute-start(bf16[2,512,256]{2,1,0:T(8,128)(2,1)S(1)} %get-tuple-element.162), channel_id=1, source_target_pairs={{0,4},{4,0},{8,12},{12,8},{16,20},{20,16},{24,28},{28,24},{1,5},{5... | collective-permute-start | bytes 1572872 | tf_op jit(solution)/shard_map/ppermute | solution.py:439
  384.6 26.1 %collective-permute-start.20 = (bf16[2,1024,256]{2,1,0:T(8,128)(2,1)S(1)}, bf16[2,1024,256]{2,1,0:T(8,128)(2,1)S(1)}, u32[]{:S(2)}, u32[]{:S(2)}) collective-permute-start(bf16[2,1024,256]{2,1,0:T(8,128)(2,1)S(1)} %get-tuple-element.160), channel_id=1, source_target_pairs={{0,2},{1,3},{2,0},{3,1},{4,6},{5,7},{6,4},{7,5},{8,10},{9,11},{10,... | collective-permute-start | bytes 3145736 | tf_op jit(solution)/shard_map/ppermute | solution.py:439
  387.6 33.6 %collective-permute-start.35 = (bf16[2,512,512]{2,1,0:T(8,128)(2,1)S(1)}, bf16[2,512,512]{2,1,0:T(8,128)(2,1)S(1)}, u32[]{:S(2)}, u32[]{:S(2)}) collective-permute-start(bf16[2,512,512]{2,1,0:T(8,128)(2,1)S(1)} %add_convert_fusion.1), channel_id=1, source_target_pairs={{0,4},{4,0},{8,12},{12,8},{16,20},{20,16},{24,28},{28,24},{1,5},{5... | collective-permute-start | bytes 3145736 | tf_op jit(solution)/shard_map/ppermute | solution.py:439
  388.4 12.7 %collective-permute-start.33 = (bf16[2,128,512]{2,1,0:T(8,128)(2,1)S(1)}, bf16[2,128,512]{2,1,0:T(8,128)(2,1)S(1)}, u32[]{:S(2)}, u32[]{:S(2)}) collective-permute-start(bf16[2,128,512]{2,1,0:T(8,128)(2,1)S(1)} %slice.247), channel_id=1, source_target_pairs={{0,16},{4,20},{8,24},{12,28},{16,0},{20,4},{24,8},{28,12},{1,17},{... | collective-permute-start | bytes 786440 | tf_op jit(solution)/shard_map/ppermute | solution.py:439
  391.2 28.1 %collective-permute-start.26 = (bf16[2,512,256]{2,1,0:T(8,128)(2,1)S(1)}, bf16[2,512,256]{2,1,0:T(8,128)(2,1)S(1)}, u32[]{:S(2)}, u32[]{:S(2)}) collective-permute-start(bf16[2,512,256]{2,1,0:T(8,128)(2,1)S(1)} %add_convert_fusion.7), channel_id=1, source_target_pairs={{0,2},{1,3},{2,0},{3,1},{4,6},{5,7},{6,4},{7,5},{8,10},{9,11},{10,... | collective-permute-start | bytes 1572872 | tf_op jit(solution)/shard_map/ppermute | solution.py:439
  410.8 22.6 %collective-permute-start.21 = (bf16[2,512,256]{2,1,0:T(8,128)(2,1)S(1)}, bf16[2,512,256]{2,1,0:T(8,128)(2,1)S(1)}, u32[]{:S(2)}, u32[]{:S(2)}) collective-permute-start(bf16[2,512,256]{2,1,0:T(8,128)(2,1)S(1)} %add_convert_fusion.9), channel_id=1, source_target_pairs={{0,4},{4,0},{8,12},{12,8},{16,20},{20,16},{24,28},{28,24},{1,5},{5... | collective-permute-start | bytes 1572872 | tf_op jit(solution)/shard_map/ppermute | solution.py:439
  419.6 6.4 %collective-permute-start.27 = (bf16[2,256,256]{2,1,0:T(8,128)(2,1)S(1)}, bf16[2,256,256]{2,1,0:T(8,128)(2,1)S(1)}, u32[]{:S(2)}, u32[]{:S(2)}) collective-permute-start(bf16[2,256,256]{2,1,0:T(8,128)(2,1)S(1)} %slice.233), channel_id=1, source_target_pairs={{0,8},{4,12},{8,0},{12,4},{16,24},{20,28},{24,16},{28,20},{1,9},{5... | collective-permute-start | bytes 786440 | tf_op jit(solution)/shard_map/ppermute | solution.py:439
  426.2 7.2 %collective-permute-start.28 = (bf16[2,128,256]{2,1,0:T(8,128)(2,1)S(1)}, bf16[2,128,256]{2,1,0:T(8,128)(2,1)S(1)}, u32[]{:S(2)}, u32[]{:S(2)}) collective-permute-start(bf16[2,128,256]{2,1,0:T(8,128)(2,1)S(1)} %slice.235), channel_id=1, source_target_pairs={{0,16},{4,20},{8,24},{12,28},{16,0},{20,4},{24,8},{28,12},{1,17},{... | collective-permute-start | bytes 393224 | tf_op jit(solution)/shard_map/ppermute | solution.py:439
  431.1 16.8 %collective-permute-start.36 = (bf16[2,256,512]{2,1,0:T(8,128)(2,1)S(1)}, bf16[2,256,512]{2,1,0:T(8,128)(2,1)S(1)}, u32[]{:S(2)}, u32[]{:S(2)}) collective-permute-start(bf16[2,256,512]{2,1,0:T(8,128)(2,1)S(1)} %slice.255), channel_id=1, source_target_pairs={{0,8},{4,12},{8,0},{12,4},{16,24},{20,28},{24,16},{28,20},{1,9},{5... | collective-permute-start | bytes 1572872 | tf_op jit(solution)/shard_map/ppermute | solution.py:439
  433.7 16.9 %collective-permute-start.22 = (bf16[2,256,256]{2,1,0:T(8,128)(2,1)S(1)}, bf16[2,256,256]{2,1,0:T(8,128)(2,1)S(1)}, u32[]{:S(2)}, u32[]{:S(2)}) collective-permute-start(bf16[2,256,256]{2,1,0:T(8,128)(2,1)S(1)} %slice.221), channel_id=1, source_target_pairs={{0,8},{4,12},{8,0},{12,4},{16,24},{20,28},{24,16},{28,20},{1,9},{5... | collective-permute-start | bytes 786440 | tf_op jit(solution)/shard_map/ppermute | solution.py:439
  448.0 12.4 %collective-permute-start.37 = (bf16[2,128,512]{2,1,0:T(8,128)(2,1)S(1)}, bf16[2,128,512]{2,1,0:T(8,128)(2,1)S(1)}, u32[]{:S(2)}, u32[]{:S(2)}) collective-permute-start(bf16[2,128,512]{2,1,0:T(8,128)(2,1)S(1)} %slice.257), channel_id=1, source_target_pairs={{0,16},{4,20},{8,24},{12,28},{16,0},{20,4},{24,8},{28,12},{1,17},{... | collective-permute-start | bytes 786440 | tf_op jit(solution)/shard_map/ppermute | solution.py:439
  450.8 11.8 %collective-permute-start.23 = (bf16[2,128,256]{2,1,0:T(8,128)(2,1)S(1)}, bf16[2,128,256]{2,1,0:T(8,128)(2,1)S(1)}, u32[]{:S(2)}, u32[]{:S(2)}) collective-permute-start(bf16[2,128,256]{2,1,0:T(8,128)(2,1)S(1)} %slice.223), channel_id=1, source_target_pairs={{0,16},{4,20},{8,24},{12,28},{16,0},{20,4},{24,8},{28,12},{1,17},{... | collective-permute-start | bytes 393224 | tf_op jit(solution)/shard_map/ppermute | solution.py:439
  (77 other events, 574.0 us)
